TPU v7x, 256 devices: a whole 4x4x8 slice. The times are simulated.
256 devices in a mesh: lon: 64 (over z, y, x_lo), lat: 4 (over x_hi, core).
Axes of the slice: x: 4 (x_hi: 2, x_lo: 2; x = x_hi * 2 + x_lo), y: 4, z: 8, core: 2. Of those that a mesh axis runs over, the one named last changes fastest.
Arguments:
- thermal_anomaly: float32 [3, 1024, 8192], P(None, 'lat', 'lon'), may hold values from -6 to 6
- saltiness_anomaly: float32 [3, 1024, 8192], P(None, 'lat', 'lon'), may hold values from -6 to 6
- zonal_transport_ratio: float32 [3, 1024, 8192], P(None, 'lat', 'lon'), may hold values from -0.15 to 0.15
- meridional_transport_ratio: float32 [3, 1024, 8192], P(None, 'lat', 'lon'), may hold values from -0.15 to 0.15
- mixing_factor: float32 [3, 1024, 8192], P(None, 'lat', 'lon'), may hold values from 0.01 to 0.08
- water_indicator: int32 [3, 1024, 8192], P(None, 'lat', 'lon'), may hold values 0 or 1
- seam_mirror_index: int32 [8192], P('lon'), may hold values from 0 to 8191, as said below
Outputs:
- new_temperature: float32 [3, 1024, 8192], P(None, 'lat', 'lon')
- new_salinity: float32 [3, 1024, 8192], P(None, 'lat', 'lon')
- density: float32 [3, 1024, 8192], P(None, 'lat', 'lon')
Inputs may be any that keep to these rules, and one draw needn't show every extreme that they name: `seam_mirror_index`: the columns are in blocks of 128; every column of block d meets a column of block (r - 1 - d) modulo 8192 / 128, with one whole number r drawn from the seed, and the columns of one block meet the columns of their partner block each exactly once.
All inputs are finite; a program needn't handle non-finite values. No bound on the sum of `water_indicator` on one device may be relied on, other than what follows from the above.
Results may differ from a plain program's by a relative error of at most 0.00002.
Values sent between devices are 32-bit elements; how exact they have to be, the bound alone decides.
No kernel may reach another device: no remote copies, remote signals or barrier semaphores. Data moves between devices by JAX's collectives and lax.ppermute only.
A program may use at most 192 MiB of HBM per device.

v0:
```python
import jax
import jax.numpy as jnp
from jax import lax
from jax.sharding import PartitionSpec as P

STEPS = 4


def extended(block, sides, width, periodic):
    for axis, dim in sides:
        count = lax.axis_size(axis)
        forward = [(i, i + 1) for i in range(count - 1)]
        if periodic:
            forward.append((count - 1, 0))
        backward = [(target, source) for source, target in forward]
        low = lax.ppermute(
            lax.slice_in_dim(block, block.shape[dim] - width, None, axis=dim), axis, forward
        )
        high = lax.ppermute(lax.slice_in_dim(block, 0, width, axis=dim), axis, backward)
        block = jnp.concatenate([low, block, high], axis=dim)
    return block


def fold_values(top_rows, partner_local):
    gathered = lax.all_gather(top_rows, "lon", axis=2, tiled=True)
    return jnp.take(gathered, partner_local, axis=2)


def extend(scalar_quantities, fold_count, partner_local):
    side = extended(scalar_quantities, (("lon", 3),), 1, True)
    westward = side[..., :-2]
    eastward = side[..., 2:]
    upright = extended(scalar_quantities, (("lat", 2),), 1, False)
    southward = upright[:, :, :-2, :]
    top_row = upright[:, :, -1, :]
    folded = fold_values(scalar_quantities[:fold_count, :, -2, :], partner_local)
    ghost_all = jnp.concatenate([folded, top_row[fold_count:]], axis=0)
    at_top = lax.axis_index("lat") == lax.axis_size("lat") - 1
    north_edge = jnp.where(at_top, ghost_all, top_row)
    northward = jnp.concatenate([scalar_quantities[:, :, 1:, :], north_edge[:, :, None, :]], axis=2)
    return (westward, eastward, southward, northward)


def face_flux(lower, upper, speed, opened, coeff):
    return opened * (
        jnp.maximum(speed, 0.0) * lower + jnp.minimum(speed, 0.0) * upper - coeff * (upper - lower)
    )


def advance(scalar_quantities, sides, sea, faces):
    (
        open_w,
        open_e,
        open_s,
        open_n,
        dif_w,
        dif_e,
        dif_s,
        dif_n,
        speed_e,
        speed_w,
        speed_n,
        speed_s,
    ) = faces
    westward, eastward, southward, northward = sides
    east_flux = face_flux(scalar_quantities, eastward, speed_e, open_e, dif_e)
    west_flux = face_flux(westward, scalar_quantities, speed_w, open_w, dif_w)
    north_flux = face_flux(scalar_quantities, northward, speed_n, open_n, dif_n)
    south_flux = face_flux(southward, scalar_quantities, speed_s, open_s, dif_s)
    return sea * (scalar_quantities - (east_flux - west_flux) - (north_flux - south_flux))


def on_device(
    thermal_anomaly,
    saltiness_anomaly,
    zonal_transport_ratio,
    meridional_transport_ratio,
    mixing_factor,
    water_indicator,
    seam_mirror_index,
):
    sea = water_indicator.astype(jnp.float32)
    static = jnp.stack([sea, mixing_factor, zonal_transport_ratio, meridional_transport_ratio])
    west_all, east_all, south_all, north_all = extend(static, 2, seam_mirror_index)
    faces = (
        west_all[0] * sea,
        sea * east_all[0],
        south_all[0] * sea,
        sea * north_all[0],
        0.5 * (west_all[1] + mixing_factor),
        0.5 * (mixing_factor + east_all[1]),
        0.5 * (south_all[1] + mixing_factor),
        0.5 * (mixing_factor + north_all[1]),
        zonal_transport_ratio,
        west_all[2],
        meridional_transport_ratio,
        south_all[3],
    )
    scalar_quantities = jnp.stack([thermal_anomaly, saltiness_anomaly])
    for step in range(STEPS):
        scalar_quantities = advance(
            scalar_quantities, extend(scalar_quantities, 2, seam_mirror_index), sea, faces
        )
    heat = scalar_quantities[0]
    salt_new = scalar_quantities[1]
    density = sea * (-0.2 * heat * (1.0 + 0.05 * heat) + 0.8 * salt_new - 0.01 * heat * salt_new)
    return (heat, salt_new, density)


def solution(mesh):
    in_specs = (
        P(None, "lat", "lon"),
        P(None, "lat", "lon"),
        P(None, "lat", "lon"),
        P(None, "lat", "lon"),
        P(None, "lat", "lon"),
        P(None, "lat", "lon"),
        P("lon"),
    )
    out_specs = (P(None, "lat", "lon"), P(None, "lat", "lon"), P(None, "lat", "lon"))
    return jax.shard_map(
        on_device, mesh=mesh, in_specs=in_specs, out_specs=out_specs, check_vma=False
    )
```

profile of v0, /device:TPU:1, one launch (start us, length us, event | category | flops | bytes accessed | tf_op | source)
XLA Modules:
  0.0 1038.5 jit_solution(15982381367545721453)
XLA Ops:
  0.6 1.8 fusion.66
  3.8 2.2 fusion.59
  6.0 2.6 copy.1250
  8.6 2.0 collective-permute-start.2
  11.2 5.2 collective-permute-start.6
  16.4 1.9 collective-permute-start.4
  18.3 2.5 copy.1246
  20.8 6.9 collective-permute-start
  30.6 1.9 collective-permute-start.5
  34.9 2.6 fusion
  40.0 135.5 %all-gather = f32[2,3,1,8192]{3,2,1,0:T(1,128)} all-gather(f32[2,3,1,128]{3,2,1,0:T(1,128)S(1)} %pad_maximum_fusion.38), channel_id=2, replica_groups=mesh['lon'=64,'lat'=4] {'lon'}, dimensions={3}, use_global_device_ids=true | all-gather | bytes 199680 | tf_op jit(solution)/shard_map/all_gather | solution.py:25
  175.5 9.1 copy.1293
  187.1 4.9 gather_fusion
  192.0 1.8 select_bitcast_fusion
  193.7 133.6 %all-gather.1 = f32[2,3,1,8192]{3,0,2,1:T(2,128)} all-gather(f32[2,3,1,128]{3,0,2,1:T(2,128)} %copy.1309), channel_id=3, replica_groups=mesh['lon'=64,'lat'=4] {'lon'}, dimensions={3}, use_global_device_ids=true | all-gather | bytes 199680 | tf_op jit(solution)/shard_map/all_gather | solution.py:25
  329.6 9.2 copy.1259
  338.9 4.3 gather_fusion.1
  348.2 2.1 fusion.43
  350.3 61.6 %collective-permute-start.7 = (f32[2,3,1,128]{3,2,1,0:T(1,128)S(1)}, f32[2,3,1,128]{3,2,1,0:T(1,128)S(1)}, u32[]{:S(2)}, u32[]{:S(2)}) collective-permute-start(f32[2,3,1,128]{3,2,1,0:T(1,128)S(1)} %copy-done.37), channel_id=1, source_target_pairs={{0,1},{1,2},{2,3},{4,5},{5,6},{6,7},{8,9},{9,10},{10,11},{12,13},{... | collective-permute-start | bytes 9224 | tf_op jit(solution)/shard_map/ppermute | solution.py:16
  415.5 2.3 fusion.47
  419.1 2.5 copy.1247
  421.8 1.7 fusion.51
  423.6 1.5 minimum_bitcast_fusion
  425.6 1.6 subtract_multiply_fusion
  429.0 1.9 collective-permute-start.10
  430.9 138.2 %all-gather.2 = f32[2,3,1,8192]{3,0,2,1:T(2,128)} all-gather(f32[2,3,1,128]{3,0,2,1:T(2,128)S(1)} %copy.1267), channel_id=4, replica_groups=mesh['lon'=64,'lat'=4] {'lon'}, dimensions={3}, use_global_device_ids=true | all-gather | bytes 199680 | tf_op jit(solution)/shard_map/all_gather | solution.py:25
  570.0 9.1 copy.1268
  579.1 4.9 gather_fusion.2
  587.9 33.7 %collective-permute-start.11 = (f32[2,3,1,128]{3,2,1,0:T(1,128)}, f32[2,3,1,128]{3,2,1,0:T(1,128)}, u32[]{:S(2)}, u32[]{:S(2)}) collective-permute-start(f32[2,3,1,128]{3,2,1,0:T(1,128)} %get-tuple-element.53), channel_id=1, source_target_pairs={{0,1},{1,2},{2,3},{4,5},{5,6},{6,7},{8,9},{9,10},{10,11},{12,13},{... | collective-permute-start | bytes 9224 | tf_op jit(solution)/shard_map/ppermute | solution.py:16
  623.7 1.9 copy.1264
  626.9 3.8 fusion.28
  632.4 1.9 collective-permute-start.14
  634.3 137.4 %all-gather.3 = f32[2,3,1,8192]{3,0,2,1:T(2,128)} all-gather(f32[2,3,1,128]{3,0,2,1:T(2,128)S(1)} %copy.1277), channel_id=5, replica_groups=mesh['lon'=64,'lat'=4] {'lon'}, dimensions={3}, use_global_device_ids=true | all-gather | bytes 199680 | tf_op jit(solution)/shard_map/all_gather | solution.py:25
  772.6 9.1 copy.1278
  781.7 4.9 gather_fusion.3
  790.4 33.3 %collective-permute-start.15 = (f32[2,3,1,128]{3,2,1,0:T(1,128)}, f32[2,3,1,128]{3,2,1,0:T(1,128)}, u32[]{:S(2)}, u32[]{:S(2)}) collective-permute-start(f32[2,3,1,128]{3,2,1,0:T(1,128)} %get-tuple-element.48), channel_id=1, source_target_pairs={{0,1},{1,2},{2,3},{4,5},{5,6},{6,7},{8,9},{9,10},{10,11},{12,13},{... | collective-permute-start | bytes 9224 | tf_op jit(solution)/shard_map/ppermute | solution.py:16
  825.7 1.9 copy.1274
  828.8 3.8 fusion.19
  834.4 1.9 collective-permute-start.18
  836.3 137.0 %all-gather.4 = f32[2,3,1,8192]{3,0,2,1:T(2,128)} all-gather(f32[2,3,1,128]{3,0,2,1:T(2,128)S(1)} %copy.1287), channel_id=6, replica_groups=mesh['lon'=64,'lat'=4] {'lon'}, dimensions={3}, use_global_device_ids=true | all-gather | bytes 199680 | tf_op jit(solution)/shard_map/all_gather | solution.py:25
  974.2 9.1 copy.1288
  983.3 4.9 gather_fusion.4
  988.5 2.0 copy.1285
  992.0 33.7 %collective-permute-start.19 = (f32[2,3,1,128]{3,2,1,0:T(1,128)}, f32[2,3,1,128]{3,2,1,0:T(1,128)S(1)}, u32[]{:S(2)}, u32[]{:S(2)}) collective-permute-start(f32[2,3,1,128]{3,2,1,0:T(1,128)} %get-tuple-element.43), channel_id=1, source_target_pairs={{0,1},{1,2},{2,3},{4,5},{5,6},{6,7},{8,9},{9,10},{10,11},{12,13},{... | collective-permute-start | bytes 9224 | tf_op jit(solution)/shard_map/ppermute | solution.py:16
  1027.1 1.8 fusion.52
  1029.9 1.9 copy.1284
  1031.9 1.9 copy.1286
  1033.8 3.7 fusion.10
  (155 shorter events, 52.2 us)
Async XLA Ops:
  6.0 4.6 copy-start
  6.0 4.6 copy-start.1
  6.0 4.6 copy-start.2
  8.6 19.1 %copy-start.24 = (f32[3,256,128]{2,1,0:T(8,128)S(1)}, f32[3,256,128]{2,1,0:T(8,128)}, u32[]{:S(2)}) copy-start(f32[3,256,128]{2,1,0:T(8,128)} %param.10) | copy-start | bytes 1179652
  8.6 405.7 %collective-permute-start.2 = (f32[4,3,256,1]{2,0,3,1:T(4,128)}, f32[4,3,256,1]{2,0,3,1:T(4,128)}, u32[]{:S(2)}, u32[]{:S(2)}) collective-permute-start(f32[4,3,256,1]{2,0,3,1:T(4,128)} %copy.1250), channel_id=1, source_target_pairs={{0,4},{4,8},{8,12},{12,16},{16,20},{20,24},{24,28},{28,32},{32,36}... | collective-permute-start | bytes 36872 | tf_op jit(solution)/shard_map/ppermute | solution.py:16
  11.2 404.3 %collective-permute-start.6 = (f32[4,3,1,128]{3,2,1,0:T(1,128)}, f32[4,3,1,128]{3,2,1,0:T(1,128)S(1)}, u32[]{:S(2)}, u32[]{:S(2)}) collective-permute-start(f32[4,3,1,128]{3,2,1,0:T(1,128)} %get-tuple-element.39), channel_id=1, source_target_pairs={{0,1},{1,2},{2,3},{4,5},{5,6},{6,7},{8,9},{9,10},{10,11},{12,13},{... | collective-permute-start | bytes 18440 | tf_op jit(solution)/shard_map/ppermute | solution.py:16
  16.4 331.2 %collective-permute-start.4 = (f32[4,3,1,128]{3,2,1,0:T(1,128)}, f32[4,3,1,128]{3,2,1,0:T(1,128)S(1)}, u32[]{:S(2)}, u32[]{:S(2)}) collective-permute-start(f32[4,3,1,128]{3,2,1,0:T(1,128)} %get-tuple-element.38), channel_id=1, source_target_pairs={{1,0},{2,1},{3,2},{5,4},{6,5},{7,6},{9,8},{10,9},{11,10},{13,12},{... | collective-permute-start | bytes 18440 | tf_op jit(solution)/shard_map/ppermute | solution.py:19
  20.8 398.3 %collective-permute-start = (f32[4,3,256,1]{2,0,3,1:T(4,128)}, f32[4,3,256,1]{2,0,3,1:T(4,128)}, u32[]{:S(2)}, u32[]{:S(2)}) collective-permute-start(f32[4,3,256,1]{2,0,3,1:T(4,128)} %copy.1246), channel_id=1, source_target_pairs={{4,0},{8,4},{12,8},{16,12},{20,16},{24,20},{28,24},{32,28},{36,32}... | collective-permute-start | bytes 36872 | tf_op jit(solution)/shard_map/ppermute | solution.py:19
  30.6 314.3 %collective-permute-start.5 = (f32[2,3,1,128]{1,0,3,2:T(2,128)}, f32[2,3,1,128]{1,0,3,2:T(2,128)}, u32[]{:S(2)}, u32[]{:S(2)}) collective-permute-start(f32[2,3,1,128]{1,0,3,2:T(2,128)} %copy.1260), channel_id=1, source_target_pairs={{1,0},{2,1},{3,2},{5,4},{6,5},{7,6},{9,8},{10,9},{11,10},{13,12},{... | collective-permute-start | bytes 9224 | tf_op jit(solution)/shard_map/ppermute | solution.py:19
  329.6 14.9 %copy-start.29 = (f32[2,3,256,1]{3,2,1,0:T(8,128)S(1)}, f32[2,3,256,1]{3,2,1,0:T(8,128)}, u32[]{:S(2)}) copy-start(f32[2,3,256,1]{3,2,1,0:T(8,128)} %get-tuple-element.56) | copy-start | bytes 18436
  338.9 7.0 copy-start.34
  338.9 9.3 copy-start.21
  344.8 5.4 collective-permute-start.1
  347.6 65.5 %collective-permute-start.3 = (f32[2,3,256,1]{2,0,3,1:T(2,128)S(1)}, f32[2,3,256,1]{2,0,3,1:T(2,128)S(1)}, u32[]{:S(2)}, u32[]{:S(2)}) collective-permute-start(f32[2,3,256,1]{2,0,3,1:T(2,128)S(1)} %copy.1308), channel_id=1, source_target_pairs={{0,4},{4,8},{8,12},{12,16},{16,20},{20,24},{24,28},{28,32},{32,36}... | collective-permute-start | bytes 18440 | tf_op jit(solution)/shard_map/ppermute | solution.py:16
  350.3 74.8 %collective-permute-start.7 = (f32[2,3,1,128]{3,2,1,0:T(1,128)S(1)}, f32[2,3,1,128]{3,2,1,0:T(1,128)S(1)}, u32[]{:S(2)}, u32[]{:S(2)}) collective-permute-start(f32[2,3,1,128]{3,2,1,0:T(1,128)S(1)} %copy-done.37), channel_id=1, source_target_pairs={{0,1},{1,2},{2,3},{4,5},{5,6},{6,7},{8,9},{9,10},{10,11},{12,13},{... | collective-permute-start | bytes 9224 | tf_op jit(solution)/shard_map/ppermute | solution.py:16
  419.1 2.5 copy-start.22
  419.1 4.5 copy-start.33
  419.1 6.0 copy-start.32
  421.7 3.5 copy-start.7
  421.7 3.5 copy-start.9
  421.7 3.5 copy-start.13
  421.7 3.5 copy-start.14
  421.7 3.5 copy-start.15
  421.7 3.5 copy-start.16
  421.7 3.5 copy-start.17
  421.7 3.5 copy-start.26
  421.7 3.5 copy-start.28
  421.7 3.5 copy-start.30
  421.7 3.5 copy-start.31
  423.5 3.7 copy-start.18
  423.5 3.7 copy-start.19
  423.5 3.7 copy-start.20
  429.0 192.7 %collective-permute-start.10 = (f32[2,3,1,128]{3,2,1,0:T(1,128)S(1)}, f32[2,3,1,128]{3,2,1,0:T(1,128)}, u32[]{:S(2)}, u32[]{:S(2)}) collective-permute-start(f32[2,3,1,128]{3,2,1,0:T(1,128)S(1)} %get-tuple-element.54), channel_id=1, source_target_pairs={{1,0},{2,1},{3,2},{5,4},{6,5},{7,6},{9,8},{10,9},{11,10},{13,12},{... | collective-permute-start | bytes 9224 | tf_op jit(solution)/shard_map/ppermute | solution.py:19
  579.1 43.4 %copy-start.35 = (pred[128]{0:T(512)(128)(4,1)S(1)}, pred[128]{0:T(512)(128)(4,1)}, u32[]{:S(2)}) copy-start(pred[128]{0:T(512)(128)(4,1)} %compare_and_fusion) | copy-start | bytes 388
  585.4 38.3 %collective-permute-start.8 = (f32[2,3,256,1]{2,0,3,1:T(2,128)S(1)}, f32[2,3,256,1]{2,0,3,1:T(2,128)}, u32[]{:S(2)}, u32[]{:S(2)}) collective-permute-start(f32[2,3,256,1]{2,0,3,1:T(2,128)S(1)} %copy.1263), channel_id=1, source_target_pairs={{4,0},{8,4},{12,8},{16,12},{20,16},{24,20},{28,24},{32,28},{36,32}... | collective-permute-start | bytes 18440 | tf_op jit(solution)/shard_map/ppermute | solution.py:19
  586.5 39.2 %collective-permute-start.9 = (f32[2,3,256,1]{2,0,3,1:T(2,128)}, f32[2,3,256,1]{2,0,3,1:T(2,128)S(1)}, u32[]{:S(2)}, u32[]{:S(2)}) collective-permute-start(f32[2,3,256,1]{2,0,3,1:T(2,128)} %copy.1265), channel_id=1, source_target_pairs={{0,4},{4,8},{8,12},{12,16},{16,20},{20,24},{24,28},{28,32},{32,36}... | collective-permute-start | bytes 18440 | tf_op jit(solution)/shard_map/ppermute | solution.py:16
  587.9 38.9 %collective-permute-start.11 = (f32[2,3,1,128]{3,2,1,0:T(1,128)}, f32[2,3,1,128]{3,2,1,0:T(1,128)}, u32[]{:S(2)}, u32[]{:S(2)}) collective-permute-start(f32[2,3,1,128]{3,2,1,0:T(1,128)} %get-tuple-element.53), channel_id=1, source_target_pairs={{0,1},{1,2},{2,3},{4,5},{5,6},{6,7},{8,9},{9,10},{10,11},{12,13},{... | collective-permute-start | bytes 9224 | tf_op jit(solution)/shard_map/ppermute | solution.py:16
  632.4 191.3 %collective-permute-start.14 = (f32[2,3,1,128]{3,2,1,0:T(1,128)S(1)}, f32[2,3,1,128]{3,2,1,0:T(1,128)}, u32[]{:S(2)}, u32[]{:S(2)}) collective-permute-start(f32[2,3,1,128]{3,2,1,0:T(1,128)S(1)} %get-tuple-element.49), channel_id=1, source_target_pairs={{1,0},{2,1},{3,2},{5,4},{6,5},{7,6},{9,8},{10,9},{11,10},{13,12},{... | collective-permute-start | bytes 9224 | tf_op jit(solution)/shard_map/ppermute | solution.py:19
  788.0 37.7 %collective-permute-start.12 = (f32[2,3,256,1]{2,0,3,1:T(2,128)S(1)}, f32[2,3,256,1]{2,0,3,1:T(2,128)}, u32[]{:S(2)}, u32[]{:S(2)}) collective-permute-start(f32[2,3,256,1]{2,0,3,1:T(2,128)S(1)} %copy.1273), channel_id=1, source_target_pairs={{4,0},{8,4},{12,8},{16,12},{20,16},{24,20},{28,24},{32,28},{36,32}... | collective-permute-start | bytes 18440 | tf_op jit(solution)/shard_map/ppermute | solution.py:19
  788.9 38.7 %collective-permute-start.13 = (f32[2,3,256,1]{2,0,3,1:T(2,128)}, f32[2,3,256,1]{2,0,3,1:T(2,128)S(1)}, u32[]{:S(2)}, u32[]{:S(2)}) collective-permute-start(f32[2,3,256,1]{2,0,3,1:T(2,128)} %copy.1275), channel_id=1, source_target_pairs={{0,4},{4,8},{8,12},{12,16},{16,20},{20,24},{24,28},{28,32},{32,36}... | collective-permute-start | bytes 18440 | tf_op jit(solution)/shard_map/ppermute | solution.py:16
  790.4 38.4 %collective-permute-start.15 = (f32[2,3,1,128]{3,2,1,0:T(1,128)}, f32[2,3,1,128]{3,2,1,0:T(1,128)}, u32[]{:S(2)}, u32[]{:S(2)}) collective-permute-start(f32[2,3,1,128]{3,2,1,0:T(1,128)} %get-tuple-element.48), channel_id=1, source_target_pairs={{0,1},{1,2},{2,3},{4,5},{5,6},{6,7},{8,9},{9,10},{10,11},{12,13},{... | collective-permute-start | bytes 9224 | tf_op jit(solution)/shard_map/ppermute | solution.py:16
  834.4 191.3 %collective-permute-start.18 = (f32[2,3,1,128]{3,2,1,0:T(1,128)}, f32[2,3,1,128]{3,2,1,0:T(1,128)}, u32[]{:S(2)}, u32[]{:S(2)}) collective-permute-start(f32[2,3,1,128]{3,2,1,0:T(1,128)} %get-tuple-element.44), channel_id=1, source_target_pairs={{1,0},{2,1},{3,2},{5,4},{6,5},{7,6},{9,8},{10,9},{11,10},{13,12},{... | collective-permute-start | bytes 9224 | tf_op jit(solution)/shard_map/ppermute | solution.py:19
  988.5 45.3 %copy-start.8 = (f32[3,256,128]{2,1,0:T(8,128)S(1)}, f32[3,256,128]{2,1,0:T(8,128)}, u32[]{:S(2)}) copy-start(f32[3,256,128]{2,1,0:T(8,128)} %get-tuple-element.36) | copy-start | bytes 1179652
  988.5 45.3 %copy-start.10 = (f32[3,256,128]{2,1,0:T(8,128)S(1)}, f32[3,256,128]{2,1,0:T(8,128)}, u32[]{:S(2)}) copy-start(f32[3,256,128]{2,1,0:T(8,128)} %get-tuple-element.60) | copy-start | bytes 1179652
  988.5 41.5 %collective-permute-start.16 = (f32[2,3,256,1]{2,0,3,1:T(2,128)S(1)}, f32[2,3,256,1]{2,0,3,1:T(2,128)}, u32[]{:S(2)}, u32[]{:S(2)}) collective-permute-start(f32[2,3,256,1]{2,0,3,1:T(2,128)S(1)} %copy.1283), channel_id=1, source_target_pairs={{4,0},{8,4},{12,8},{16,12},{20,16},{24,20},{28,24},{32,28},{36,32}... | collective-permute-start | bytes 18440 | tf_op jit(solution)/shard_map/ppermute | solution.py:19
  990.6 41.3 %collective-permute-start.17 = (f32[2,3,256,1]{2,0,3,1:T(2,128)}, f32[2,3,256,1]{2,0,3,1:T(2,128)}, u32[]{:S(2)}, u32[]{:S(2)}) collective-permute-start(f32[2,3,256,1]{2,0,3,1:T(2,128)} %copy.1285), channel_id=1, source_target_pairs={{0,4},{4,8},{8,12},{12,16},{16,20},{20,24},{24,28},{28,32},{32,36}... | collective-permute-start | bytes 18440 | tf_op jit(solution)/shard_map/ppermute | solution.py:16
  992.0 41.8 %collective-permute-start.19 = (f32[2,3,1,128]{3,2,1,0:T(1,128)}, f32[2,3,1,128]{3,2,1,0:T(1,128)S(1)}, u32[]{:S(2)}, u32[]{:S(2)}) collective-permute-start(f32[2,3,1,128]{3,2,1,0:T(1,128)} %get-tuple-element.43), channel_id=1, source_target_pairs={{0,1},{1,2},{2,3},{4,5},{5,6},{6,7},{8,9},{9,10},{10,11},{12,13},{... | collective-permute-start | bytes 9224 | tf_op jit(solution)/shard_map/ppermute | solution.py:16
  1033.8 3.7 copy-start.23
  (10 other events, 18.6 us)
where the time goes:
time: 1040 us
  blocking collectives  682 us (66%)
  starting transfers between devices  192 us (18%)
  local copies, waits for them, and re-layouts  120 us (12%)
  other arithmetic  43.1 us (4%)
    all_gather x5, blocking collectives, fold_values(): gathered = lax.all_gather(top_rows, 'lon', axis=2, tiled=True)  682 us
    ppermute x10, starting transfers between devices, extended(): lax.ppermute(lax.slice_in_dim(block, block.shape[dim] - width, None, axis...  174 us
    all_gather x5, local copies, waits for them, and re-layouts, fold_values(): gathered = lax.all_gather(top_rows, 'lon', axis=2, tiled=True)  45.7 us
    gather x5, local copies, waits for them, and re-layouts, fold_values(): return jnp.take(gathered, partner_local, axis=2)  23.9 us
  transfers between devices with their start and end apart: 20, of which 0 were waited for; matrix products, arithmetic and copies ran while one was open for 13% of the time, Pallas kernels for 0%

commit v1 on v0

v1 whole, which is shorter than its diff:
```python
import functools

import jax
import jax.numpy as jnp
from jax import lax
from jax.experimental import pallas as pl
from jax.experimental.pallas import tpu as pltpu
from jax.sharding import PartitionSpec as P

STEPS = 4
LEVELS = 3
ROWS = 256
COLS = 128
LON = 64
LAT = 4
AXES = ("lon", "lat")
HALF = LON // 2

BASE = 16
NORTH = BASE + ROWS
EXT = 288
FIRST_BLOCK = 8
BLOCKS = 34

TILES = 23


def flat(lon, lat):
    return (lon % LON) * LAT + lat


def lon_pairs(partner):
    return [(flat(i, a), flat(partner(i), a)) for i in range(LON) for a in range(LAT)]


PAIR_X = lon_pairs(lambda i: i ^ 1)
PAIR_Y = lon_pairs(lambda i: ((i - 1) ^ 1) + 1)
PAIR_A = [(flat(i, a), flat(i, a ^ 1)) for i in range(LON) for a in range(LAT)]
PAIR_B = [(flat(i, a), flat(i, 3 - a)) for i in range(LON) for a in (1, 2)]


def fold_pairs(r):
    top = [(flat(i, 3), flat(r - 1 - i, 3)) for i in range(LON)]
    relay = [(flat(i, 2), flat(r + HALF - 1 - i, 2)) for i in range(LON)]
    return top + relay


def swap(x, pairs):
    return lax.ppermute(x, AXES, pairs)


def iota(axis):
    return lax.broadcasted_iota(jnp.int32, (8, COLS), axis)


def roll(x, shift, axis=1):
    return pltpu.roll(x, shift % x.shape[axis], axis)


def sea_of(x):
    return x.astype(jnp.float32)


def vmem(n):
    return [pl.BlockSpec(memory_space=pltpu.VMEM)] * n


def whole(rows):
    return pl.BlockSpec((rows, COLS), lambda i: (0, 0))


PARAMS = pltpu.CompilerParams(vmem_limit_bytes=48 << 20)


def pack_kernel(t_ref, s_ref, u_ref, v_ref, k_ref, w_ref, m_ref, xs_ref, ys_ref, pt_ref, pc_ref):
    odd = lax.rem(lax.axis_index("lon"), 2) == 1
    lane = iota(1)
    group = lane >> 3
    low = (lane & 7) < 4

    def block(i, carry):
        rows = pl.ds(pl.multiple_of(i * 8, 8), 8)
        tracers = jnp.zeros((8, COLS), jnp.float32)
        for t, ref in enumerate((t_ref, s_ref)):
            for l in range(LEVELS):
                j = 3 * t + l
                tracers = jnp.where(group == j, roll(ref[l, rows, :], 4 + 8 * j), tracers)
        coefs = jnp.zeros((8, COLS), jnp.float32)
        for f, ref in enumerate((u_ref, v_ref, k_ref, w_ref)):
            for l in range(LEVELS):
                j = 3 * f + l
                x = ref[l, rows, :]
                if f == 3:
                    x = sea_of(x)
                coefs = jnp.where(group == j, roll(x, 4 + 8 * j), coefs)
        pt_ref[rows, :] = tracers
        pc_ref[rows, :] = coefs
        east = jnp.where(low, coefs, roll(tracers, 4))
        west = jnp.where(low, roll(tracers, -4), coefs)
        xs_ref[rows, :] = jnp.where(odd, west, east)
        ys_ref[rows, :] = jnp.where(odd, east, west)
        return carry

    lax.fori_loop(0, ROWS // 8, block, 0, unroll=4)
    second = ROWS - 2
    for out in (xs_ref, ys_ref):
        for l in range(LEVELS):
            one = slice(second, second + 1)
            out[pl.ds(256 + l, 1), :] = t_ref[l, one, :]
            out[pl.ds(259 + l, 1), :] = s_ref[l, one, :]
            out[pl.ds(262 + l, 1), :] = sea_of(w_ref[l, one, :])
            out[pl.ds(265 + l, 1), :] = k_ref[l, one, :]
        out[pl.ds(268, 1), :] = m_ref[...].astype(jnp.float32)
        out[pl.ds(269, 3), :] = jnp.zeros((3, COLS), jnp.float32)


def pack(t, s, u, v, k, w, m):
    edge = jax.ShapeDtypeStruct((ROWS + 16, COLS), jnp.float32)
    own = jax.ShapeDtypeStruct((ROWS, COLS), jnp.float32)
    return pl.pallas_call(
        pack_kernel,
        out_shape=(edge, edge, own, own),
        in_specs=vmem(7),
        out_specs=tuple(vmem(4)),
        compiler_params=PARAMS,
        name="pack",
    )(t, s, u, v, k, w, m)


def strips(pt, pc, mw, me):
    lane = iota(1)
    low = (lane & 7) < 4
    wt = jnp.where(low, roll(mw, -4), pt)
    et = jnp.where(low, pt, roll(me, 4))
    wc = jnp.where(low, mw, pc)
    ec = jnp.where(low, pc, me)
    out = [jnp.where(lane < 48, wt, roll(et, 48))]
    for f in range(4):
        west = jnp.where(lane < 24, roll(wc, -24 * f), roll(wc, 24 - 24 * f))
        east = jnp.where(lane < 72, roll(ec, 48 - 24 * f), roll(ec, 72 - 24 * f))
        out.append(jnp.where(lane < 48, west, east))
    return out


def rows_kernel(*refs):
    south = refs[0:6]
    north = refs[6:12]
    pts, ptn, pcs, pcn, xrs, xrn, yrs, yrn, xre, yre, m_ref = refs[12:23]
    a_ref, b_ref, f_ref = refs[23:26]
    odd = lax.rem(lax.axis_index("lon"), 2) == 1
    odd_lat = lax.rem(lax.axis_index("lat"), 2) == 1

    def tiles(fields, pt, pc, xr, yr):
        x, y = xr[...], yr[...]
        mw, me = jnp.where(odd, x, y), jnp.where(odd, y, x)
        out = []
        for f, ref in enumerate(fields):
            for l in range(LEVELS):
                x = ref[l]
                out.append(sea_of(x) if f == 5 else x)
        return out + strips(pt[...], pc[...], mw, me)

    top = tiles(north, ptn, pcn, xrn, yrn)
    bottom = tiles(south, pts, pcs, xrs, yrs)
    for j in range(TILES):
        f_ref[pl.ds(8 * j, 8), :] = top[j]
        up, down = top[j][4:8, :], bottom[j][0:4, :]
        a_ref[pl.ds(4 * j, 4), :] = jnp.where(odd_lat, down, up)
        b_ref[pl.ds(4 * j, 4), :] = jnp.where(odd_lat, up, down)
    a_ref[pl.ds(4 * TILES, 4), :] = jnp.zeros((4, COLS), jnp.float32)
    b_ref[pl.ds(4 * TILES, 4), :] = jnp.zeros((4, COLS), jnp.float32)
    x, y = xre[...], yre[...]
    ew, ee = jnp.where(odd, x, y), jnp.where(odd, y, x)
    row = iota(0)
    own = jnp.broadcast_to(m_ref[...].astype(jnp.float32), (8, COLS))
    west = jnp.broadcast_to(ew[4:5, :], (8, COLS))
    east = jnp.broadcast_to(ee[4:5, :], (8, COLS))
    f_ref[pl.ds(8 * TILES, 8), :] = jnp.where(row == 0, own, jnp.where(row == 1, west, east))


def rows(fields, pt, pc, xr, yr, m):
    last = ROWS // 8 - 1
    low3 = pl.BlockSpec((LEVELS, 8, COLS), lambda i: (0, 0, 0))
    top3 = pl.BlockSpec((LEVELS, 8, COLS), lambda i: (0, last, 0))
    low = pl.BlockSpec((8, COLS), lambda i: (0, 0))
    top = pl.BlockSpec((8, COLS), lambda i: (last, 0))
    extra = pl.BlockSpec((8, COLS), lambda i: (last + 2, 0))
    msg = jax.ShapeDtypeStruct((4 * TILES + 4, COLS), jnp.float32)
    return pl.pallas_call(
        rows_kernel,
        out_shape=(msg, msg, jax.ShapeDtypeStruct((8 * TILES + 8, COLS), jnp.float32)),
        grid=(1,),
        in_specs=[low3] * 6
        + [top3] * 6
        + [low, top] * 4
        + [extra, extra, pl.BlockSpec((1, COLS), lambda i: (0, 0))],
        out_specs=(whole(4 * TILES + 4), whole(4 * TILES + 4), whole(8 * TILES + 8)),
        compiler_params=PARAMS,
        name="rows",
    )(*fields, *fields, pt, pt, pc, pc, xr, xr, yr, yr, xr, yr, m)


def coefficients(k, s, u, v, kn, ke, ks, kw, sn, se, ss, sw, uw, vs):
    zero = jnp.zeros_like(k)
    fe, fw, fn, fs = 0.5 * (k + ke), 0.5 * (kw + k), 0.5 * (k + kn), 0.5 * (ks + k)
    oe, ow, on, os = s * se, sw * s, s * sn, ss * s
    ae, be = oe * (jnp.maximum(u, zero) + fe), oe * (jnp.minimum(u, zero) - fe)
    aw, bw = ow * (jnp.maximum(uw, zero) + fw), ow * (jnp.minimum(uw, zero) - fw)
    an, bn = on * (jnp.maximum(v, zero) + fn), on * (jnp.minimum(v, zero) - fn)
    a_s, bs = os * (jnp.maximum(vs, zero) + fs), os * (jnp.minimum(vs, zero) - fs)
    centre = s - (ae - bw) - (an - bs)
    return centre, -be, aw, -bn, a_s


def stencil(c, q, e, w, n, s):
    return c[0] * q + c[1] * e + c[2] * w + c[3] * n + c[4] * s


def edges(strip):
    return jnp.where((iota(1) & 7) == 3, strip, roll(strip, -50))


def beside(x, edge, j):
    lane = iota(1)
    z = roll(edge, -(8 * j + 3))
    return jnp.where(lane == COLS - 1, z, roll(x, -1)), jnp.where(lane == 0, z, roll(x, 1))


def gather(x, index):
    return jnp.take_along_axis(x, index, axis=1)


def ghost_kernel(p_ref, d_ref, xe_ref, ye_ref, g_ref):
    odd = lax.rem(lax.axis_index("lon"), 2) == 1
    row, lane = iota(0), iota(1)
    top = row == 7

    def tile(ref, j):
        return ref[pl.ds(8 * j, 8), :]

    def spread(index_row):
        return jnp.broadcast_to(index_row.astype(jnp.int32) & (COLS - 1), (8, COLS))

    index_d = spread(d_ref[pl.ds(8 * TILES, 1), :])
    index_p = spread(p_ref[pl.ds(8 * TILES, 1), :])
    index_pw = spread(p_ref[pl.ds(8 * TILES + 1, 1), :])
    index_pe = spread(p_ref[pl.ds(8 * TILES + 2, 1), :])
    xe0, ye0 = xe_ref[pl.ds(0, 8), :], ye_ref[pl.ds(0, 8), :]
    xe1, ye1 = xe_ref[pl.ds(8, 8), :], ye_ref[pl.ds(8, 8), :]
    east = [gather(jnp.where(odd, y, x), index_pw) for x, y in ((xe0, ye0), (xe1, ye1))]
    west = [gather(jnp.where(odd, x, y), index_pe) for x, y in ((xe0, ye0), (xe1, ye1))]

    def outer(kind):
        out = jnp.zeros((8, COLS), jnp.float32)
        for j in range(6):
            n = (j, 6 + j % 3, 9 + j % 3)[kind]
            w = jnp.broadcast_to(east[n // 8][n % 8 : n % 8 + 1, :], (8, COLS))
            e = jnp.broadcast_to(west[n // 8][n % 8 : n % 8 + 1, :], (8, COLS))
            out = jnp.where((lane >> 3) == j, roll(w, 8 * j + 4), out)
            out = jnp.where((lane >> 3) == j + 6, roll(e, 8 * j + 52), out)
        return out

    def north(x, ghost):
        return jnp.where(top, ghost, roll(x, -1, 0))

    def below(x):
        return roll(x, 1, 0)

    def field(ref, f, l):
        return tile(ref, 3 * f + l)

    def fold(x, index):
        return roll(gather(x, index), 1, 0)

    def coefs(ref, ghosts, strip_ghosts):
        out = []
        ek, es, eu = (edges(tile(ref, 18 + f)) for f in (3, 4, 1))
        for l in range(LEVELS):
            u, v, k, s = (field(ref, f, l) for f in (2, 3, 4, 5))
            ke, kw = beside(k, ek, l)
            se, sw = beside(s, es, l)
            uw = beside(u, eu, l)[1]
            gs, gk = ghosts[l]
            out.append(coefficients(k, s, u, v, north(k, gk), ke, below(k), kw, north(s, gs), se, below(s), sw, uw, below(v)))
        u, v, k, s = (tile(ref, 18 + f) for f in (1, 2, 3, 4))
        gs, gk = strip_ghosts
        out.append(
            coefficients(
                k, s, u, v, north(k, gk), roll(k, -1), below(k), roll(k, 1), north(s, gs), roll(s, -1), below(s), roll(s, 1),
                roll(u, 1), below(v),
            )
        )
        return out

    def advance(c, q, strip, ghosts, strip_ghost):
        edge = edges(strip)
        out = []
        for j in range(6):
            e, w = beside(q[j], edge, j)
            out.append(stencil(c[j % 3], q[j], e, w, north(q[j], ghosts[j]), below(q[j])))
        new = stencil(c[3], strip, roll(strip, -1), roll(strip, 1), north(strip, strip_ghost), below(strip))
        return out, new

    zero = jnp.zeros((8, COLS), jnp.float32)
    d0 = [tile(d_ref, j) for j in range(6)]
    p0 = [tile(p_ref, j) for j in range(6)]
    static = [(fold(field(d_ref, 5, l), index_p), fold(field(d_ref, 4, l), index_p)) for l in range(LEVELS)]
    cp = coefs(p_ref, static, (outer(1), outer(2)))
    cd = coefs(d_ref, [(zero, zero)] * 3, (zero, zero))
    d1, _ = advance(cd, d0, tile(d_ref, 18), [zero] * 6, zero)
    p1, strip = advance(cp, p0, tile(p_ref, 18), [fold(x, index_p) for x in d0], outer(0))
    p2, strip = advance(cp, p1, strip, [fold(x, index_p) for x in d1], zero)
    p3, _ = advance(cp, p2, strip, [zero] * 6, zero)
    for j in range(6):
        l = j % 3
        values = [p0[j], p1[j], p2[j], p3[j], field(p_ref, 5, l), field(p_ref, 4, l)]
        out = zero
        for i, x in enumerate(values):
            out = jnp.where(row == i, roll(gather(x, index_d), i - 6, 0), out)
        g_ref[pl.ds(8 * j, 8), :] = out


def ghosts(partner, own, xr, yr):
    extra = pl.BlockSpec((16, COLS), lambda i: (ROWS // 16, 0))
    return pl.pallas_call(
        ghost_kernel,
        out_shape=jax.ShapeDtypeStruct((48, COLS), jnp.float32),
        grid=(1,),
        in_specs=[whole(8 * TILES + 8)] * 2 + [extra, extra],
        out_specs=whole(48),
        compiler_params=PARAMS,
        name="ghost",
    )(partner, own, xr, yr)


def steps_kernel(*refs):
    t_ref, s_ref, u_ref, v_ref, k_ref, w_ref, pt_ref, pc_ref, xr_ref, yr_ref, a_ref, b_ref, g_ref, gx_ref, gy_ref = refs[:15]
    heat_ref, salt_ref, dens_ref = refs[15:18]
    q0, q1, fields, coef = refs[18:22]
    odd = lax.rem(lax.axis_index("lon"), 2) == 1
    lat = lax.axis_index("lat")
    odd_lat = lax.rem(lat, 2) == 1
    at_top = lat == LAT - 1
    lane = iota(1)
    tracers = (t_ref, s_ref)

    def fill(i, carry):
        src = pl.ds(pl.multiple_of(i * 8, 8), 8)
        dst = pl.ds(pl.multiple_of(i * 8 + BASE, 8), 8)
        for t in range(2):
            for l in range(LEVELS):
                q0[3 * t + l, dst, :] = tracers[t][l, src, :]
        for f, ref in enumerate((u_ref, v_ref, k_ref, w_ref)):
            for l in range(LEVELS):
                x = ref[l, src, :]
                fields[4 * f + l, dst, :] = sea_of(x) if f == 3 else x
        x, y = xr_ref[src, :], yr_ref[src, :]
        mw, me = jnp.where(odd, x, y), jnp.where(odd, y, x)
        parts = strips(pt_ref[src, :], pc_ref[src, :], mw, me)
        q0[6, dst, :] = parts[0]
        for f in range(4):
            fields[4 * f + 3, dst, :] = parts[1 + f]
        return carry

    lax.fori_loop(0, ROWS // 8, fill, 0, unroll=2)

    def place(j):
        if j < 6:
            return q0, j
        if j < 18:
            return fields, 4 * ((j - 6) // 3) + j % 3
        if j == 18:
            return q0, 6
        return fields, 4 * (j - 19) + 3

    for j in range(TILES):
        a, b = a_ref[pl.ds(4 * j, 4), :], b_ref[pl.ds(4 * j, 4), :]
        ref, n = place(j)
        ref[n, pl.ds(BASE - 4, 4), :] = jnp.where(odd_lat, a, b)
        ref[n, pl.ds(NORTH, 4), :] = jnp.where(odd_lat, b, a)

    own = [g_ref[pl.ds(8 * j, 8), :] for j in range(6)]
    strip = jnp.zeros((8, COLS), jnp.float32)
    for j in range(6):
        x, y = gx_ref[pl.ds(8 * j, 8), :], gy_ref[pl.ds(8 * j, 8), :]
        west, east = jnp.where(odd, x, y), jnp.where(odd, y, x)
        strip = jnp.where((lane >> 3) == j, roll(jnp.where(lane >= COLS - 4, west, own[j]), 8 * j + 4), strip)
        strip = jnp.where((lane >> 3) == j + 6, roll(jnp.where(lane < 4, east, own[j]), 8 * j + 52), strip)

    def put(ref, s):
        @pl.when(at_top)
        def _():
            for j in range(6):
                ref[j, pl.ds(NORTH, 1), :] = own[j][s : s + 1, :]
            ref[6, pl.ds(NORTH, 1), :] = strip[s : s + 1, :]

    put(q0, 0)

    @pl.when(at_top)
    def _():
        for f, s in ((3, 4), (2, 5)):
            for l in range(LEVELS):
                fields[4 * f + l, pl.ds(NORTH, 1), :] = own[l][s : s + 1, :]
            fields[4 * f + 3, pl.ds(NORTH, 1), :] = strip[s : s + 1, :]

    def coef_block(i, carry):
        r = i * 8 + FIRST_BLOCK

        def load(f, l, shift=0):
            return fields[4 * f + l, pl.ds(r + shift, 8), :]

        ku, ks, kk = (edges(load(f, 3)) for f in (0, 3, 2))
        for l in range(4):
            u, v, k, s = (load(f, l) for f in range(4))
            if l < 3:
                ke, kw = beside(k, kk, l)
                se, sw = beside(s, ks, l)
                uw = beside(u, ku, l)[1]
            else:
                ke, kw, se, sw, uw = roll(k, -1), roll(k, 1), roll(s, -1), roll(s, 1), roll(u, 1)
            out = coefficients(
                k, s, u, v, load(2, l, 1), ke, load(2, l, -1), kw, load(3, l, 1), se, load(3, l, -1), sw, uw, load(1, l, -1)
            )
            for n in range(5):
                coef[4 * n + l, pl.ds(pl.multiple_of(r, 8), 8), :] = out[n]
        return carry

    lax.fori_loop(0, BLOCKS, coef_block, 0)

    def advance(src, r):
        rows = pl.ds(pl.multiple_of(r, 8), 8)
        strip = src[6, rows, :]
        edge = edges(strip)
        out = []
        for j in range(6):
            c = [coef[4 * n + j % 3, rows, :] for n in range(5)]
            q = src[j, rows, :]
            e, w = beside(q, edge, j)
            out.append(stencil(c, q, e, w, src[j, pl.ds(r + 1, 8), :], src[j, pl.ds(r - 1, 8), :]))
        return out, strip

    def step(src, dst):
        def block(i, carry):
            r = i * 8 + FIRST_BLOCK
            rows = pl.ds(pl.multiple_of(r, 8), 8)
            out, strip = advance(src, r)
            for j in range(6):
                dst[j, rows, :] = out[j]
            c = [coef[4 * n + 3, rows, :] for n in range(5)]
            dst[6, rows, :] = stencil(
                c, strip, roll(strip, -1), roll(strip, 1), src[6, pl.ds(r + 1, 8), :], src[6, pl.ds(r - 1, 8), :]
            )
            return carry

        lax.fori_loop(0, BLOCKS, block, 0)

    step(q0, q1)
    put(q1, 1)
    step(q1, q0)
    put(q0, 2)
    step(q0, q1)
    put(q1, 3)

    def final(i, carry):
        out, _ = advance(q1, i * 8 + BASE)
        dst = pl.ds(pl.multiple_of(i * 8, 8), 8)
        for l in range(LEVELS):
            heat, salt = out[l], out[3 + l]
            sea = sea_of(w_ref[l, dst, :])
            heat_ref[l, dst, :] = heat
            salt_ref[l, dst, :] = salt
            dens_ref[l, dst, :] = sea * (-0.2 * heat * (1.0 + 0.05 * heat) + 0.8 * salt - 0.01 * heat * salt)
        return carry

    lax.fori_loop(0, ROWS // 8, final, 0)


def four_steps(*operands):
    out = jax.ShapeDtypeStruct((LEVELS, ROWS, COLS), jnp.float32)
    return pl.pallas_call(
        steps_kernel,
        out_shape=(out, out, out),
        in_specs=vmem(len(operands)),
        out_specs=tuple(vmem(3)),
        scratch_shapes=[
            pltpu.VMEM((7, EXT, COLS), jnp.float32),
            pltpu.VMEM((7, EXT, COLS), jnp.float32),
            pltpu.VMEM((16, EXT, COLS), jnp.float32),
            pltpu.VMEM((20, EXT, COLS), jnp.float32),
        ],
        compiler_params=PARAMS,
        name="steps",
    )(*operands)


def fold_exchange(message, seam):
    rotation = (seam[0] // COLS + 1 + lax.axis_index("lon")) % LON
    far = rotation >= HALF

    def relay(x):
        return lax.cond(far, lambda y: swap(y, PAIR_A), lambda y: y, x)

    branches = [functools.partial(swap, pairs=fold_pairs(r)) for r in range(HALF)]
    return relay(lax.switch(rotation % HALF, branches, relay(message)))


def on_device(t, s, u, v, k, w, seam):
    m = seam.reshape(1, COLS)
    xs, ys, pt, pc = pack(t, s, u, v, k, w, m)
    yr = swap(ys, PAIR_Y)
    xr = swap(xs, PAIR_X)
    a, b, message = rows((t, s, u, v, k, w), pt, pc, xr, yr, m)
    partner = fold_exchange(message, seam)
    ar = swap(a, PAIR_A)
    br = swap(b, PAIR_B)
    g = ghosts(partner, message, xr, yr)
    gy = swap(g, PAIR_Y)
    gx = swap(g, PAIR_X)
    return four_steps(t, s, u, v, k, w, pt, pc, xr, yr, ar, br, g, gx, gy)


def solution(mesh):
    block = P(None, "lat", "lon")
    return jax.shard_map(
        on_device,
        mesh=mesh,
        in_specs=(block,) * 6 + (P("lon"),),
        out_specs=(block,) * 3,
        check_vma=False,
    )
```

time: 1040 us -> 91.9 us (0.09)
  the two profiles are of different devices: /device:TPU:1 before, /device:TPU:4 now
where the time goes in v1:
time: 91.9 us; the launch traced here: 91.3 us
  starting transfers between devices  37.8 us (41%)
  Pallas kernels  32.1 us (35%)
  waiting for transfers between devices  13.1 us (14%)
  local copies, waits for them, and re-layouts  7.29 us (8%)
  between operations  0.92 us (1%)
    ppermute x9, starting transfers between devices, swap(): return lax.ppermute(x, AXES, pairs)  37.8 us
    pallas_call x1, Pallas kernels, four_steps(): pl.pallas_call(steps_kernel, out_shape=(out, out, out), in_specs=vmem(len...  29 us
    ppermute x9, waiting for transfers between devices, swap(): return lax.ppermute(x, AXES, pairs)  13.1 us
    unnamed x26, local copies, waits for them, and re-layouts  6.64 us
  transfers between devices with their start and end apart: 9, of which 6 were waited for; matrix products, arithmetic and copies ran while one was open for 1% of the time, Pallas kernels for 2%

profile of v1, /device:TPU:4, one launch (start us, length us, event | category | flops | bytes accessed | tf_op | source)
XLA Modules:
  0.0 91.3 jit_solution(14518225447271281658)
XLA Ops:
  0.6 0.0 copy-start.12
  0.6 0.6 copy-done.12
  1.3 0.0 copy-start
  1.3 1.0 %copy-done = f32[3,256,128]{2,1,0:T(8,128)S(1)} copy-done((f32[3,256,128]{2,1,0:T(8,128)S(1)}, f32[3,256,128]{2,1,0:T(8,128)}, u32[]{:S(2)}) %copy-start) | copy-done | bytes 393240
  2.3 0.0 copy-start.2
  2.3 1.0 %copy-done.2 = f32[3,256,128]{2,1,0:T(8,128)S(1)} copy-done((f32[3,256,128]{2,1,0:T(8,128)S(1)}, f32[3,256,128]{2,1,0:T(8,128)}, u32[]{:S(2)}) %copy-start.2) | copy-done | bytes 393240
  3.3 0.0 copy-start.4
  3.3 1.0 %copy-done.4 = f32[3,256,128]{2,1,0:T(8,128)S(1)} copy-done((f32[3,256,128]{2,1,0:T(8,128)S(1)}, f32[3,256,128]{2,1,0:T(8,128)}, u32[]{:S(2)}) %copy-start.4) | copy-done | bytes 393240
  4.3 0.0 copy-start.6
  4.3 1.0 %copy-done.6 = f32[3,256,128]{2,1,0:T(8,128)S(1)} copy-done((f32[3,256,128]{2,1,0:T(8,128)S(1)}, f32[3,256,128]{2,1,0:T(8,128)}, u32[]{:S(2)}) %copy-start.6) | copy-done | bytes 393240
  5.3 0.0 copy-start.8
  5.3 1.0 %copy-done.8 = f32[3,256,128]{2,1,0:T(8,128)S(1)} copy-done((f32[3,256,128]{2,1,0:T(8,128)S(1)}, f32[3,256,128]{2,1,0:T(8,128)}, u32[]{:S(2)}) %copy-start.8) | copy-done | bytes 393240
  6.3 1.0 %copy-done.10 = s32[3,256,128]{2,1,0:T(8,128)S(1)} copy-done((s32[3,256,128]{2,1,0:T(8,128)S(1)}, s32[3,256,128]{2,1,0:T(8,128)}, u32[]{:S(2)}) %copy-start.10) | copy-done | bytes 393240
  7.3 1.4 %pack.1 = (f32[272,128]{1,0:T(8,128)S(1)}, f32[272,128]{1,0:T(8,128)S(1)}, f32[256,128]{1,0:T(8,128)S(1)}, f32[256,128]{1,0:T(8,128)S(1)}) custom-call(f32[3,256,128]{2,1,0:T(8,128)S(1)} %copy-done, f32[3,256,128]{2,1,0:T(8,128)S(1)} %copy-done.2, f32[3,256,128]{2,1,0:T(8,128)S(1)} %copy-done.4, f32[3,256,128]{2,1,0:T(8,128)S(1)} %copy-done.6, ...), custom_call_target="tpu_custom_call" | custom-call | tf_op jit(solution)/shard_map/pack/pallas_call | solution.py:120
  8.6 1.3 %collective-permute-start.34 = (f32[272,128]{1,0:T(8,128)S(1)}, f32[272,128]{1,0:T(8,128)S(1)}, u32[]{:S(2)}, u32[]{:S(2)}) collective-permute-start(f32[272,128]{1,0:T(8,128)S(1)} %get-tuple-element.87), channel_id=1, source_target_pairs={{0,4},{1,5},{2,6},{3,7},{4,0},{5,1},{6,2},{7,3},{8,12},{9,13},{10,... | collective-permute-start | bytes 417800 | tf_op jit(solution)/shard_map/ppermute | solution.py:49
  9.9 8.6 %collective-permute-start.35 = (f32[272,128]{1,0:T(8,128)S(1)}, f32[272,128]{1,0:T(8,128)S(1)}, u32[]{:S(2)}, u32[]{:S(2)}) collective-permute-start(f32[272,128]{1,0:T(8,128)S(1)} %get-tuple-element.88), channel_id=1, source_target_pairs={{0,252},{1,253},{2,254},{3,255},{4,8},{5,9},{6,10},{7,11},{8,4},{9... | collective-permute-start | bytes 417800 | tf_op jit(solution)/shard_map/ppermute | solution.py:49
  18.5 0.0 collective-permute-done.34.refs_16_.refs_17_.refs_20_.xe_ref.refs_8_
  18.5 3.4 %collective-permute-done.35.refs_18_.refs_19_.refs_21_.ye_ref.refs_9_ = f32[272,128]{1,0:T(8,128)S(1)} collective-permute-done((f32[272,128]{1,0:T(8,128)S(1)}, f32[272,128]{1,0:T(8,128)S(1)}, u32[]{:S(2)}, u32[]{:S(2)}) %collective-permute-start.35) | collective-permute-done | bytes 139296 | tf_op jit(solution)/shard_map/ppermute | solution.py:49
  21.9 0.0 copy-start.5
  21.9 0.0 copy-start.7
  21.9 0.2 rows.1
  22.1 8.5 %collective-permute-start.36 = (f32[96,128]{1,0:T(8,128)S(1)}, f32[96,128]{1,0:T(8,128)S(1)}, u32[]{:S(2)}, u32[]{:S(2)}) collective-permute-start(f32[96,128]{1,0:T(8,128)S(1)} %get-tuple-element.89), channel_id=1, source_target_pairs={{0,1},{1,0},{2,3},{3,2},{4,5},{5,4},{6,7},{7,6},{8,9},{9,8},{10,11... | collective-permute-start | bytes 147464 | tf_op jit(solution)/shard_map/ppermute | solution.py:49
  30.6 2.0 %collective-permute-start.37 = (f32[96,128]{1,0:T(8,128)S(1)}, f32[96,128]{1,0:T(8,128)S(1)}, u32[]{:S(2)}, u32[]{:S(2)}) collective-permute-start(f32[96,128]{1,0:T(8,128)S(1)} %get-tuple-element.90), channel_id=1, source_target_pairs={{1,2},{2,1},{5,6},{6,5},{9,10},{10,9},{13,14},{14,13},{17,18},{18,... | collective-permute-start | bytes 147464 | tf_op jit(solution)/shard_map/ppermute | solution.py:49
  32.8 0.0 copy-start.3
  32.8 1.5 %conditional.3 = (f32[192,128]{1,0:T(8,128)}) conditional(s32[]{:T(128)} %convert_element_type.4, f32[192,128]{1,0:T(8,128)S(1)} %get-tuple-element.91.d_ref, f32[192,128]{1,0:T(8,128)S(1)} %get-tuple-element.91.d_ref), branch_computations={%region_0.1_spmd, %region_1.2_spmd} | conditional | bytes 393264 | solution.py:501
  32.8 0.1 collective-permute-start
  32.9 1.4 %collective-permute-done = f32[192,128]{1,0:T(8,128)} collective-permute-done((f32[192,128]{1,0:T(8,128)S(1)}, f32[192,128]{1,0:T(8,128)}, u32[]{:S(2)}, u32[]{:S(2)}) %collective-permute-start) | collective-permute-done | bytes 98336 | tf_op jit(solution)/shard_map/cond/branch_1_fun/ppermute | solution.py:49
  34.4 15.4 %conditional.4 = (f32[192,128]{1,0:T(8,128)}) conditional(s32[]{:T(128)} %clamp.3, f32[192,128]{1,0:T(8,128)} %get-tuple-element.92, f32[192,128]{1,0:T(8,128)} %get-tuple-element.92, f32[192,128]{1,0:T(8,128)} %get-tuple-element.92, f32[192,128]{1,0:T(8,128)} %get-tuple-element.92, ...), branch_computations={%region_2.3_spmd, %region_3.4_spmd, %region_4.5_spmd, %region_5.6_... | conditional | bytes 393264 | solution.py:504
  34.4 12.4 %collective-permute-start.9 = (f32[192,128]{1,0:T(8,128)}, f32[192,128]{1,0:T(8,128)}, u32[]{:S(2)}, u32[]{:S(2)}) collective-permute-start(f32[192,128]{1,0:T(8,128)} %param.10), channel_id=1, source_target_pairs={{3,31},{7,27},{11,23},{15,19},{19,15},{23,11},{27,7},{31,3},{35,25... | collective-permute-start | bytes 294920 | tf_op jit(solution)/shard_map/cond/branch_8_fun/ppermute | solution.py:49
  46.7 3.0 %collective-permute-done.9 = f32[192,128]{1,0:T(8,128)} collective-permute-done((f32[192,128]{1,0:T(8,128)}, f32[192,128]{1,0:T(8,128)}, u32[]{:S(2)}, u32[]{:S(2)}) %collective-permute-start.9) | collective-permute-done | bytes 98336 | tf_op jit(solution)/shard_map/cond/branch_8_fun/ppermute | solution.py:49
  49.7 2.2 %conditional.5 = (f32[192,128]{1,0:T(8,128)}) conditional(s32[]{:T(128)} %convert_element_type.4, f32[192,128]{1,0:T(8,128)} %get-tuple-element.93, f32[192,128]{1,0:T(8,128)} %get-tuple-element.93), branch_computations={%region_34.35_spmd, %region_35.36_spmd} | conditional | bytes 589872 | solution.py:501
  49.7 0.0 collective-permute-start.33
  49.7 1.5 %collective-permute-done.33 = f32[192,128]{1,0:T(8,128)S(1)} collective-permute-done((f32[192,128]{1,0:T(8,128)}, f32[192,128]{1,0:T(8,128)S(1)}, u32[]{:S(2)}, u32[]{:S(2)}) %collective-permute-start.33) | collective-permute-done | bytes 98336 | tf_op jit(solution)/shard_map/cond/branch_1_fun/ppermute | solution.py:49
  51.3 0.6 copy.45
  51.9 1.5 %ghost.1.refs_12_ = f32[48,128]{1,0:T(8,128)S(1)} custom-call(f32[192,128]{1,0:T(8,128)} %get-tuple-element.94.p_ref, f32[192,128]{1,0:T(8,128)S(1)} %get-tuple-element.91.d_ref, f32[272,128]{1,0:T(8,128)S(1)} %collective-permute-done.34.refs_16_.refs_17_.refs_20_.xe_ref.refs_8_, f32[272,128]{1,0:T(8,128)S(1)} %collective-permute-done.35.refs_18_.refs_19_.refs_21_.ye_ref.refs_9_), custom_call_target="tpu_custom_call" | custom-call | tf_op jit(solution)/shard_map/ghost/pallas_call | solution.py:325
  53.4 5.0 %collective-permute-start.39 = (f32[48,128]{1,0:T(8,128)S(1)}, f32[48,128]{1,0:T(8,128)S(1)}, u32[]{:S(2)}, u32[]{:S(2)}) collective-permute-start(f32[48,128]{1,0:T(8,128)S(1)} %ghost.1.refs_12_), channel_id=1, source_target_pairs={{0,252},{1,253},{2,254},{3,255},{4,8},{5,9},{6,10},{7,11},{8,4},{9... | collective-permute-start | bytes 73736 | tf_op jit(solution)/shard_map/ppermute | solution.py:49
  58.4 0.0 collective-permute-start.38
  58.4 3.2 %collective-permute-done.39.refs_14_ = f32[48,128]{1,0:T(8,128)S(1)} collective-permute-done((f32[48,128]{1,0:T(8,128)S(1)}, f32[48,128]{1,0:T(8,128)S(1)}, u32[]{:S(2)}, u32[]{:S(2)}) %collective-permute-start.39) | collective-permute-done | bytes 24608 | tf_op jit(solution)/shard_map/ppermute | solution.py:49
  61.6 0.7 collective-permute-done.38.refs_13_
  62.2 0.0 collective-permute-done.36.refs_10_
  62.2 0.0 collective-permute-done.37.refs_11_
  62.2 0.0 copy-done.5
  62.3 0.0 copy-done.7
  62.3 0.0 copy-done.9
  62.3 0.0 copy-done.11
  62.3 0.0 copy-done.3
  62.3 0.0 copy-done.1
  62.3 29.0 %steps.1 = (f32[3,256,128]{2,1,0:T(8,128)}, f32[3,256,128]{2,1,0:T(8,128)}, f32[3,256,128]{2,1,0:T(8,128)}) custom-call(f32[3,256,128]{2,1,0:T(8,128)S(1)} %copy-done.1, f32[3,256,128]{2,1,0:T(8,128)S(1)} %copy-done.3, f32[3,256,128]{2,1,0:T(8,128)S(1)} %copy-done.5, f32[3,256,128]{2,1,0:T(8,128)S(1)} %copy-done.7, f32[3,256,128]{2,1,0:T(8,128)S(1)} %copy-done.9, ...), custom_call_target="tpu_custom_call" | custom-call | tf_op jit(solution)/shard_map/steps/pallas_call | solution.py:480
  (4 shorter events, 0.0 us)
Async XLA Ops:
  0.6 0.7 copy-start.12
  1.3 1.0 %copy-start = (f32[3,256,128]{2,1,0:T(8,128)S(1)}, f32[3,256,128]{2,1,0:T(8,128)}, u32[]{:S(2)}) copy-start(f32[3,256,128]{2,1,0:T(8,128)} %refs_0_.3) | copy-start | bytes 1179652
  2.3 1.0 %copy-start.2 = (f32[3,256,128]{2,1,0:T(8,128)S(1)}, f32[3,256,128]{2,1,0:T(8,128)}, u32[]{:S(2)}) copy-start(f32[3,256,128]{2,1,0:T(8,128)} %refs_1_.3) | copy-start | bytes 1179652
  3.3 1.0 %copy-start.4 = (f32[3,256,128]{2,1,0:T(8,128)S(1)}, f32[3,256,128]{2,1,0:T(8,128)}, u32[]{:S(2)}) copy-start(f32[3,256,128]{2,1,0:T(8,128)} %refs_2_.3) | copy-start | bytes 1179652
  4.3 1.0 %copy-start.6 = (f32[3,256,128]{2,1,0:T(8,128)S(1)}, f32[3,256,128]{2,1,0:T(8,128)}, u32[]{:S(2)}) copy-start(f32[3,256,128]{2,1,0:T(8,128)} %refs_3_.3) | copy-start | bytes 1179652
  5.3 1.0 %copy-start.8 = (f32[3,256,128]{2,1,0:T(8,128)S(1)}, f32[3,256,128]{2,1,0:T(8,128)}, u32[]{:S(2)}) copy-start(f32[3,256,128]{2,1,0:T(8,128)} %refs_4_.3) | copy-start | bytes 1179652
  6.3 1.0 %copy-start.10 = (s32[3,256,128]{2,1,0:T(8,128)S(1)}, s32[3,256,128]{2,1,0:T(8,128)}, u32[]{:S(2)}) copy-start(s32[3,256,128]{2,1,0:T(8,128)} %refs_5_.3) | copy-start | bytes 1179652
  8.6 9.9 %collective-permute-start.34 = (f32[272,128]{1,0:T(8,128)S(1)}, f32[272,128]{1,0:T(8,128)S(1)}, u32[]{:S(2)}, u32[]{:S(2)}) collective-permute-start(f32[272,128]{1,0:T(8,128)S(1)} %get-tuple-element.87), channel_id=1, source_target_pairs={{0,4},{1,5},{2,6},{3,7},{4,0},{5,1},{6,2},{7,3},{8,12},{9,13},{10,... | collective-permute-start | bytes 417800 | tf_op jit(solution)/shard_map/ppermute | solution.py:49
  9.9 12.0 %collective-permute-start.35 = (f32[272,128]{1,0:T(8,128)S(1)}, f32[272,128]{1,0:T(8,128)S(1)}, u32[]{:S(2)}, u32[]{:S(2)}) collective-permute-start(f32[272,128]{1,0:T(8,128)S(1)} %get-tuple-element.88), channel_id=1, source_target_pairs={{0,252},{1,253},{2,254},{3,255},{4,8},{5,9},{6,10},{7,11},{8,4},{9... | collective-permute-start | bytes 417800 | tf_op jit(solution)/shard_map/ppermute | solution.py:49
  21.9 40.4 %copy-start.5 = (f32[3,256,128]{2,1,0:T(8,128)S(1)}, f32[3,256,128]{2,1,0:T(8,128)}, u32[]{:S(2)}) copy-start(f32[3,256,128]{2,1,0:T(8,128)} %refs_2_.3) | copy-start | bytes 1179652
  21.9 40.4 %copy-start.7 = (f32[3,256,128]{2,1,0:T(8,128)S(1)}, f32[3,256,128]{2,1,0:T(8,128)}, u32[]{:S(2)}) copy-start(f32[3,256,128]{2,1,0:T(8,128)} %refs_3_.3) | copy-start | bytes 1179652
  21.9 40.4 %copy-start.9 = (f32[3,256,128]{2,1,0:T(8,128)S(1)}, f32[3,256,128]{2,1,0:T(8,128)}, u32[]{:S(2)}) copy-start(f32[3,256,128]{2,1,0:T(8,128)} %refs_4_.3) | copy-start | bytes 1179652
  21.9 40.4 %copy-start.11 = (s32[3,256,128]{2,1,0:T(8,128)S(1)}, s32[3,256,128]{2,1,0:T(8,128)}, u32[]{:S(2)}) copy-start(s32[3,256,128]{2,1,0:T(8,128)} %refs_5_.3) | copy-start | bytes 1179652
  22.1 40.2 %collective-permute-start.36 = (f32[96,128]{1,0:T(8,128)S(1)}, f32[96,128]{1,0:T(8,128)S(1)}, u32[]{:S(2)}, u32[]{:S(2)}) collective-permute-start(f32[96,128]{1,0:T(8,128)S(1)} %get-tuple-element.89), channel_id=1, source_target_pairs={{0,1},{1,0},{2,3},{3,2},{4,5},{5,4},{6,7},{7,6},{8,9},{9,8},{10,11... | collective-permute-start | bytes 147464 | tf_op jit(solution)/shard_map/ppermute | solution.py:49
  30.6 31.6 %collective-permute-start.37 = (f32[96,128]{1,0:T(8,128)S(1)}, f32[96,128]{1,0:T(8,128)S(1)}, u32[]{:S(2)}, u32[]{:S(2)}) collective-permute-start(f32[96,128]{1,0:T(8,128)S(1)} %get-tuple-element.90), channel_id=1, source_target_pairs={{1,2},{2,1},{5,6},{6,5},{9,10},{10,9},{13,14},{14,13},{17,18},{18,... | collective-permute-start | bytes 147464 | tf_op jit(solution)/shard_map/ppermute | solution.py:49
  32.8 29.5 %copy-start.3 = (f32[3,256,128]{2,1,0:T(8,128)S(1)}, f32[3,256,128]{2,1,0:T(8,128)}, u32[]{:S(2)}) copy-start(f32[3,256,128]{2,1,0:T(8,128)} %refs_1_.3) | copy-start | bytes 1179652
  32.8 1.5 %collective-permute-start = (f32[192,128]{1,0:T(8,128)S(1)}, f32[192,128]{1,0:T(8,128)}, u32[]{:S(2)}, u32[]{:S(2)}) collective-permute-start(f32[192,128]{1,0:T(8,128)S(1)} %param.1), channel_id=1, source_target_pairs={{0,1},{1,0},{2,3},{3,2},{4,5},{5,4},{6,7},{7,6},{8,9},{9,8},{10,11... | collective-permute-start | bytes 294920 | tf_op jit(solution)/shard_map/cond/branch_1_fun/ppermute | solution.py:49
  34.4 27.9 %copy-start.1 = (f32[3,256,128]{2,1,0:T(8,128)S(1)}, f32[3,256,128]{2,1,0:T(8,128)}, u32[]{:S(2)}) copy-start(f32[3,256,128]{2,1,0:T(8,128)} %refs_0_.3) | copy-start | bytes 1179652
  34.4 15.4 %collective-permute-start.9 = (f32[192,128]{1,0:T(8,128)}, f32[192,128]{1,0:T(8,128)}, u32[]{:S(2)}, u32[]{:S(2)}) collective-permute-start(f32[192,128]{1,0:T(8,128)} %param.10), channel_id=1, source_target_pairs={{3,31},{7,27},{11,23},{15,19},{19,15},{23,11},{27,7},{31,3},{35,25... | collective-permute-start | bytes 294920 | tf_op jit(solution)/shard_map/cond/branch_8_fun/ppermute | solution.py:49
  49.7 1.5 %collective-permute-start.33 = (f32[192,128]{1,0:T(8,128)}, f32[192,128]{1,0:T(8,128)S(1)}, u32[]{:S(2)}, u32[]{:S(2)}) collective-permute-start(f32[192,128]{1,0:T(8,128)} %param.35), channel_id=1, source_target_pairs={{0,1},{1,0},{2,3},{3,2},{4,5},{5,4},{6,7},{7,6},{8,9},{9,8},{10,11... | collective-permute-start | bytes 294920 | tf_op jit(solution)/shard_map/cond/branch_1_fun/ppermute | solution.py:49
  53.4 8.1 %collective-permute-start.39 = (f32[48,128]{1,0:T(8,128)S(1)}, f32[48,128]{1,0:T(8,128)S(1)}, u32[]{:S(2)}, u32[]{:S(2)}) collective-permute-start(f32[48,128]{1,0:T(8,128)S(1)} %ghost.1.refs_12_), channel_id=1, source_target_pairs={{0,252},{1,253},{2,254},{3,255},{4,8},{5,9},{6,10},{7,11},{8,4},{9... | collective-permute-start | bytes 73736 | tf_op jit(solution)/shard_map/ppermute | solution.py:49
  58.4 3.8 %collective-permute-start.38 = (f32[48,128]{1,0:T(8,128)S(1)}, f32[48,128]{1,0:T(8,128)S(1)}, u32[]{:S(2)}, u32[]{:S(2)}) collective-permute-start(f32[48,128]{1,0:T(8,128)S(1)} %ghost.1.refs_12_), channel_id=1, source_target_pairs={{0,4},{1,5},{2,6},{3,7},{4,0},{5,1},{6,2},{7,3},{8,12},{9,13},{10,... | collective-permute-start | bytes 73736 | tf_op jit(solution)/shard_map/ppermute | solution.py:49

commit v2 on v1

v2 whole, which is shorter than its diff:
```python
import functools

import jax
import jax.numpy as jnp
from jax import lax
from jax.experimental import pallas as pl
from jax.experimental.pallas import tpu as pltpu
from jax.sharding import PartitionSpec as P

STEPS = 4
LEVELS = 3
ROWS = 256
COLS = 128
LON = 64
LAT = 4
AXES = ("lon", "lat")
HALF = LON // 2

BASE = 16
NORTH = BASE + ROWS
EXT = 288

TILES = 23
UNROLL = 8


def flat(lon, lat):
    return (lon % LON) * LAT + lat


def lon_pairs(partner):
    return [(flat(i, a), flat(partner(i), a)) for i in range(LON) for a in range(LAT)]


PAIR_X = lon_pairs(lambda i: i ^ 1)
PAIR_Y = lon_pairs(lambda i: ((i - 1) ^ 1) + 1)
PAIR_A = [(flat(i, a), flat(i, a ^ 1)) for i in range(LON) for a in range(LAT)]
PAIR_B = [(flat(i, a), flat(i, 3 - a)) for i in range(LON) for a in (1, 2)]


def fold_pairs(r):
    top = [(flat(i, 3), flat(r - 1 - i, 3)) for i in range(LON)]
    relay = [(flat(i, 2), flat(r + HALF - 1 - i, 2)) for i in range(LON)]
    return top + relay


def swap(x, pairs):
    return lax.ppermute(x, AXES, pairs)


def iota(axis):
    return lax.broadcasted_iota(jnp.int32, (8, COLS), axis)


def roll(x, shift, axis=1):
    return pltpu.roll(x, shift % x.shape[axis], axis)


def sea_of(x):
    return x.astype(jnp.float32)


def vmem(n):
    return [pl.BlockSpec(memory_space=pltpu.VMEM)] * n


PARAMS = pltpu.CompilerParams(vmem_limit_bytes=32 << 20)


def pack_kernel(t_hbm, s_hbm, u_hbm, v_hbm, k_hbm, w_hbm, m_hbm, xs_ref, ys_ref, pt_ref, pc_ref, q_ref, f_ref, w_ref, m_ref, sems):
    odd = lax.rem(lax.axis_index("lon"), 2) == 1
    lane = iota(1)
    group = lane >> 3
    low = (lane & 7) < 4
    own = pl.ds(BASE, ROWS)

    def target(n):
        if n >= 5:
            return (w_ref, m_ref)[n - 5]
        ref = q_ref if n < 2 else f_ref
        return ref.at[pl.ds(3 * (n if n < 2 else n - 2), LEVELS), own, :]

    copies = [
        pltpu.make_async_copy(src, target(n), sems.at[n])
        for n, src in enumerate((t_hbm, s_hbm, u_hbm, v_hbm, k_hbm, w_hbm, m_hbm))
    ]
    for copy in copies:
        copy.start()

    def gathered(ref, count, rows):
        out = jnp.zeros((8, COLS), jnp.float32)
        for j in range(count):
            out = jnp.where(group == j, roll(ref[j, rows, :], 4 + 8 * j), out)
        return out

    def tracer_block(i, carry):
        rows = pl.ds(pl.multiple_of(i * 8 + BASE, 8), 8)
        pt_ref[pl.ds(pl.multiple_of(i * 8, 8), 8), :] = gathered(q_ref, 6, rows)
        return carry

    def coef_block(i, carry):
        rows = pl.ds(pl.multiple_of(i * 8, 8), 8)
        here = pl.ds(pl.multiple_of(i * 8 + BASE, 8), 8)
        for l in range(LEVELS):
            f_ref[9 + l, here, :] = sea_of(w_ref[l, rows, :])
        tracers = pt_ref[rows, :]
        coefs = gathered(f_ref, 12, here)
        pc_ref[rows, :] = coefs
        east = jnp.where(low, coefs, roll(tracers, 4))
        west = jnp.where(low, roll(tracers, -4), coefs)
        xs_ref[rows, :] = jnp.where(odd, west, east)
        ys_ref[rows, :] = jnp.where(odd, east, west)
        return carry

    copies[0].wait()
    copies[1].wait()
    lax.fori_loop(0, ROWS // 8, tracer_block, 0, unroll=8)
    for copy in copies[2:]:
        copy.wait()
    lax.fori_loop(0, ROWS // 8, coef_block, 0, unroll=4)
    second = pl.ds(BASE + ROWS - 2, 1)
    for out in (xs_ref, ys_ref):
        for n in range(6):
            out[pl.ds(ROWS + n, 1), :] = q_ref[n, second, :]
        for l in range(LEVELS):
            out[pl.ds(ROWS + 6 + l, 1), :] = f_ref[9 + l, second, :]
            out[pl.ds(ROWS + 9 + l, 1), :] = f_ref[6 + l, second, :]
        out[pl.ds(ROWS + 12, 1), :] = m_ref[...].astype(jnp.float32)
        out[pl.ds(ROWS + 13, 3), :] = jnp.zeros((3, COLS), jnp.float32)


def pack(t, s, u, v, k, w, m):
    edge = jax.ShapeDtypeStruct((ROWS + 16, COLS), jnp.float32)
    own = jax.ShapeDtypeStruct((ROWS, COLS), jnp.float32)
    return pl.pallas_call(
        pack_kernel,
        out_shape=(
            edge,
            edge,
            own,
            own,
            jax.ShapeDtypeStruct((6, EXT, COLS), jnp.float32),
            jax.ShapeDtypeStruct((12, EXT, COLS), jnp.float32),
        ),
        in_specs=[pl.BlockSpec(memory_space=pltpu.HBM)] * 7,
        out_specs=tuple(vmem(6)),
        scratch_shapes=[
            pltpu.VMEM((LEVELS, ROWS, COLS), jnp.int32),
            pltpu.VMEM((1, COLS), jnp.int32),
            pltpu.SemaphoreType.DMA((7,)),
        ],
        compiler_params=PARAMS,
        name="pack",
    )(*(pltpu.with_memory_space_constraint(x, pltpu.HBM) for x in (t, s, u, v, k, w, m)))


def strips(pt, pc, mw, me):
    lane = iota(1)
    low = (lane & 7) < 4
    wt = jnp.where(low, roll(mw, -4), pt)
    et = jnp.where(low, pt, roll(me, 4))
    wc = jnp.where(low, mw, pc)
    ec = jnp.where(low, pc, me)
    out = [jnp.where(lane < 48, wt, roll(et, 48))]
    for f in range(4):
        west = jnp.where(lane < 24, roll(wc, -24 * f), roll(wc, 24 - 24 * f))
        east = jnp.where(lane < 72, roll(ec, 48 - 24 * f), roll(ec, 72 - 24 * f))
        out.append(jnp.where(lane < 48, west, east))
    return out


def rows_kernel(q_ref, fields, pt_ref, pc_ref, xs_ref, xr_ref, yr_ref, a_ref, b_ref, f_ref):
    odd = lax.rem(lax.axis_index("lon"), 2) == 1
    odd_lat = lax.rem(lax.axis_index("lat"), 2) == 1

    def tiles(start):
        rows = pl.ds(start, 8)
        here = pl.ds(start + BASE, 8)
        x, y = xr_ref[rows, :], yr_ref[rows, :]
        mw, me = jnp.where(odd, x, y), jnp.where(odd, y, x)
        main = [q_ref[n, here, :] for n in range(6)] + [fields[n, here, :] for n in range(12)]
        return main + strips(pt_ref[rows, :], pc_ref[rows, :], mw, me)

    top = tiles(ROWS - 8)
    bottom = tiles(0)
    for j in range(TILES):
        f_ref[pl.ds(8 * j, 8), :] = top[j]
        up, down = top[j][4:8, :], bottom[j][0:4, :]
        a_ref[pl.ds(4 * j, 4), :] = jnp.where(odd_lat, down, up)
        b_ref[pl.ds(4 * j, 4), :] = jnp.where(odd_lat, up, down)
    a_ref[pl.ds(4 * TILES, 4), :] = jnp.zeros((4, COLS), jnp.float32)
    b_ref[pl.ds(4 * TILES, 4), :] = jnp.zeros((4, COLS), jnp.float32)
    x, y = xr_ref[pl.ds(ROWS + 8, 8), :], yr_ref[pl.ds(ROWS + 8, 8), :]
    ew, ee = jnp.where(odd, x, y), jnp.where(odd, y, x)
    row = iota(0)
    own = jnp.broadcast_to(xs_ref[pl.ds(ROWS + 12, 1), :], (8, COLS))
    west = jnp.broadcast_to(ew[4:5, :], (8, COLS))
    east = jnp.broadcast_to(ee[4:5, :], (8, COLS))
    f_ref[pl.ds(8 * TILES, 8), :] = jnp.where(row == 0, own, jnp.where(row == 1, west, east))


def rows(q, fields, pt, pc, xs, xr, yr):
    msg = jax.ShapeDtypeStruct((4 * TILES + 4, COLS), jnp.float32)
    return pl.pallas_call(
        rows_kernel,
        out_shape=(msg, msg, jax.ShapeDtypeStruct((8 * TILES + 8, COLS), jnp.float32)),
        in_specs=vmem(7),
        out_specs=tuple(vmem(3)),
        compiler_params=PARAMS,
        name="rows",
    )(q, fields, pt, pc, xs, xr, yr)


def coefficients(k, s, u, v, kn, ke, ks, kw, sn, se, ss, sw, uw, vs):
    zero = jnp.zeros_like(k)
    fe, fw, fn, fs = 0.5 * (k + ke), 0.5 * (kw + k), 0.5 * (k + kn), 0.5 * (ks + k)
    oe, ow, on, os = s * se, sw * s, s * sn, ss * s
    ae, be = oe * (jnp.maximum(u, zero) + fe), oe * (jnp.minimum(u, zero) - fe)
    aw, bw = ow * (jnp.maximum(uw, zero) + fw), ow * (jnp.minimum(uw, zero) - fw)
    an, bn = on * (jnp.maximum(v, zero) + fn), on * (jnp.minimum(v, zero) - fn)
    a_s, bs = os * (jnp.maximum(vs, zero) + fs), os * (jnp.minimum(vs, zero) - fs)
    centre = s - (ae - bw) - (an - bs)
    return centre, -be, aw, -bn, a_s


def stencil(c, q, e, w, n, s):
    return c[0] * q + c[1] * e + c[2] * w + c[3] * n + c[4] * s


def edges(strip):
    return jnp.where((iota(1) & 7) == 3, strip, roll(strip, -50))


def beside(x, edge, j):
    lane = iota(1)
    z = roll(edge, -(8 * j + 3))
    return jnp.where(lane == COLS - 1, z, roll(x, -1)), jnp.where(lane == 0, z, roll(x, 1))


def gather(x, index):
    return jnp.take_along_axis(x, index, axis=1)


def ghost_kernel(p_ref, d_ref, xe_ref, ye_ref, g_ref):
    odd = lax.rem(lax.axis_index("lon"), 2) == 1
    row, lane = iota(0), iota(1)
    top = row == 7

    def tile(ref, j):
        return ref[pl.ds(8 * j, 8), :]

    def spread(index_row):
        return jnp.broadcast_to(index_row.astype(jnp.int32) & (COLS - 1), (8, COLS))

    index_d = spread(d_ref[pl.ds(8 * TILES, 1), :])
    index_p = spread(p_ref[pl.ds(8 * TILES, 1), :])
    index_pw = spread(p_ref[pl.ds(8 * TILES + 1, 1), :])
    index_pe = spread(p_ref[pl.ds(8 * TILES + 2, 1), :])
    xe0, ye0 = xe_ref[pl.ds(ROWS, 8), :], ye_ref[pl.ds(ROWS, 8), :]
    xe1, ye1 = xe_ref[pl.ds(ROWS + 8, 8), :], ye_ref[pl.ds(ROWS + 8, 8), :]
    east = [gather(jnp.where(odd, y, x), index_pw) for x, y in ((xe0, ye0), (xe1, ye1))]
    west = [gather(jnp.where(odd, x, y), index_pe) for x, y in ((xe0, ye0), (xe1, ye1))]

    def outer(kind):
        out = jnp.zeros((8, COLS), jnp.float32)
        for j in range(6):
            n = (j, 6 + j % 3, 9 + j % 3)[kind]
            w = jnp.broadcast_to(east[n // 8][n % 8 : n % 8 + 1, :], (8, COLS))
            e = jnp.broadcast_to(west[n // 8][n % 8 : n % 8 + 1, :], (8, COLS))
            out = jnp.where((lane >> 3) == j, roll(w, 8 * j + 4), out)
            out = jnp.where((lane >> 3) == j + 6, roll(e, 8 * j + 52), out)
        return out

    def north(x, ghost):
        return jnp.where(top, ghost, roll(x, -1, 0))

    def below(x):
        return roll(x, 1, 0)

    def field(ref, f, l):
        return tile(ref, 3 * f + l)

    def fold(x, index):
        return roll(gather(x, index), 1, 0)

    def coefs(ref, ghosts, strip_ghosts):
        out = []
        ek, es, eu = (edges(tile(ref, 18 + f)) for f in (3, 4, 1))
        for l in range(LEVELS):
            u, v, k, s = (field(ref, f, l) for f in (2, 3, 4, 5))
            ke, kw = beside(k, ek, l)
            se, sw = beside(s, es, l)
            uw = beside(u, eu, l)[1]
            gs, gk = ghosts[l]
            out.append(coefficients(k, s, u, v, north(k, gk), ke, below(k), kw, north(s, gs), se, below(s), sw, uw, below(v)))
        u, v, k, s = (tile(ref, 18 + f) for f in (1, 2, 3, 4))
        gs, gk = strip_ghosts
        out.append(
            coefficients(
                k, s, u, v, north(k, gk), roll(k, -1), below(k), roll(k, 1), north(s, gs), roll(s, -1), below(s), roll(s, 1),
                roll(u, 1), below(v),
            )
        )
        return out

    def advance(c, q, strip, ghosts, strip_ghost):
        edge = edges(strip)
        out = []
        for j in range(6):
            e, w = beside(q[j], edge, j)
            out.append(stencil(c[j % 3], q[j], e, w, north(q[j], ghosts[j]), below(q[j])))
        new = stencil(c[3], strip, roll(strip, -1), roll(strip, 1), north(strip, strip_ghost), below(strip))
        return out, new

    zero = jnp.zeros((8, COLS), jnp.float32)
    d0 = [tile(d_ref, j) for j in range(6)]
    p0 = [tile(p_ref, j) for j in range(6)]
    static = [(fold(field(d_ref, 5, l), index_p), fold(field(d_ref, 4, l), index_p)) for l in range(LEVELS)]
    cp = coefs(p_ref, static, (outer(1), outer(2)))
    cd = coefs(d_ref, [(zero, zero)] * 3, (zero, zero))
    d1, _ = advance(cd, d0, tile(d_ref, 18), [zero] * 6, zero)
    p1, strip = advance(cp, p0, tile(p_ref, 18), [fold(x, index_p) for x in d0], outer(0))
    p2, strip = advance(cp, p1, strip, [fold(x, index_p) for x in d1], zero)
    p3, _ = advance(cp, p2, strip, [zero] * 6, zero)
    for j in range(6):
        l = j % 3
        values = [p0[j], p1[j], p2[j], p3[j], field(p_ref, 5, l), field(p_ref, 4, l)]
        out = zero
        for i, x in enumerate(values):
            out = jnp.where(row == i, roll(gather(x, index_d), i - 6, 0), out)
        g_ref[pl.ds(8 * j, 8), :] = out


def ghosts(partner, own, xr, yr):
    return pl.pallas_call(
        ghost_kernel,
        out_shape=jax.ShapeDtypeStruct((48, COLS), jnp.float32),
        in_specs=vmem(4),
        out_specs=vmem(1)[0],
        compiler_params=PARAMS,
        name="ghost",
    )(partner, own, xr, yr)


def coef_block(load, store):
    ku, ks, kk = (load(f, 4, 0) for f in (0, 3, 2))
    for l in range(4):
        u, v, k, s = (load(f, l, 0) for f in range(4))
        if l < 3:
            ke, kw = beside(k, kk, l)
            se, sw = beside(s, ks, l)
            uw = beside(u, ku, l)[1]
        else:
            ke, kw, se, sw, uw = roll(k, -1), roll(k, 1), roll(s, -1), roll(s, 1), roll(u, 1)
        out = coefficients(
            k, s, u, v, load(2, l, 1), ke, load(2, l, -1), kw, load(3, l, 1), se, load(3, l, -1), sw, uw, load(1, l, -1)
        )
        for n in range(5):
            store(n, l, out[n])


def advance(load, c, last):
    edge = load(7, 0)
    out = []
    for j in range(6):
        q = load(j, 0)
        e, w = beside(q, edge, j)
        out.append(stencil([c(n, j % 3) for n in range(5)], q, e, w, load(j, 1), load(j, -1)))
    if not last:
        strip = load(6, 0)
        strip_c = [c(n, 3) for n in range(5)]
        new = stencil(strip_c, strip, roll(strip, -1), roll(strip, 1), load(6, 1), load(6, -1))
        out += [new, edges(new)]
    return out


def outputs(out, sea, store):
    for l in range(LEVELS):
        heat, salt = out[l], out[3 + l]
        dens = sea(l) * (-0.2 * heat * (1.0 + 0.05 * heat) + 0.8 * salt - 0.01 * heat * salt)
        for n, x in enumerate((heat, salt, dens)):
            store(n, l, x)


def eight(r):
    return pl.ds(pl.multiple_of(r, 8), 8)


def main_kernel(q_ref, fields, pt_ref, pc_ref, xr_ref, yr_ref, heat_ref, salt_ref, dens_ref, strip_ref, edge_ref, coef, qa, qb):
    odd = lax.rem(lax.axis_index("lon"), 2) == 1
    results = (heat_ref, salt_ref, dens_ref)

    def fill(i, carry):
        src = eight(i * 8)
        x, y = xr_ref[src, :], yr_ref[src, :]
        mw, me = jnp.where(odd, x, y), jnp.where(odd, y, x)
        for n, part in enumerate(strips(pt_ref[src, :], pc_ref[src, :], mw, me)):
            strip_ref[n, eight(i * 8 + BASE), :] = part
            if n != 2:
                edge_ref[n, eight(i * 8 + BASE), :] = edges(part)
        return carry

    lax.fori_loop(0, ROWS // 8, fill, 0, unroll=UNROLL)

    def block(i, carry):
        r = i * 8 + BASE

        def load(f, l, shift):
            rows = pl.ds(r + shift, 8)
            if l == 4:
                return edge_ref[1 + f, rows, :]
            return strip_ref[1 + f, rows, :] if l == 3 else fields[3 * f + l, rows, :]

        def store(n, l, x):
            coef[4 * n + l, eight(r), :] = x

        coef_block(load, store)
        return carry

    lax.fori_loop(0, ROWS // 8, block, 0, unroll=4)

    def loader(src, r):
        def load(j, shift):
            rows = pl.ds(r + shift, 8)
            if src is not None:
                return src[j, rows, :]
            return q_ref[j, rows, :] if j < 6 else (strip_ref, edge_ref)[j - 6][0, rows, :]

        return load

    def coefficient(r):
        return lambda n, l: coef[4 * n + l, eight(r), :]

    for src, dst in ((None, qa), (qa, qb), (qb, qa)):

        def block(i, carry):
            r = i * 8 + BASE
            for j, x in enumerate(advance(loader(src, r), coefficient(r), False)):
                dst[j, eight(r), :] = x
            return carry

        lax.fori_loop(0, ROWS // 8, block, 0, unroll=UNROLL)

    def final(i, carry):
        r = i * 8 + BASE
        rows = eight(i * 8)

        def store(n, l, x):
            results[n][l, rows, :] = x

        outputs(advance(loader(qa, r), coefficient(r), True), lambda l: fields[9 + l, eight(r), :], store)
        return carry

    lax.fori_loop(0, ROWS // 8, final, 0, unroll=UNROLL)


def inner_steps(q, fields, pt, pc, xr, yr):
    out = jax.ShapeDtypeStruct((LEVELS, ROWS, COLS), jnp.float32)
    return pl.pallas_call(
        main_kernel,
        out_shape=(out, out, out, jax.ShapeDtypeStruct((5, EXT, COLS), jnp.float32)),
        in_specs=vmem(6),
        out_specs=tuple(vmem(4)),
        scratch_shapes=[
            pltpu.VMEM((5, EXT, COLS), jnp.float32),
            pltpu.VMEM((20, EXT, COLS), jnp.float32),
            pltpu.VMEM((8, EXT, COLS), jnp.float32),
            pltpu.VMEM((8, EXT, COLS), jnp.float32),
        ],
        compiler_params=PARAMS,
        cost_estimate=pl.CostEstimate(flops=60_000_000, bytes_accessed=36_000_000, transcendentals=0),
        name="main",
    )(q, fields, pt, pc, xr, yr)


ZONE = 64
SHIFT = NORTH - 48
SOUTH_BLOCKS = (8, 16, 24)
NORTH_BLOCKS = (32, 40, 48)


def zone_kernel(q_ref, fields, strip_ref, a_ref, b_ref, g_ref, gx_ref, gy_ref, h_in, s_in, d_in, h_out, s_out, d_out, *scratch):
    zq, zr, zf, zc, patch, sems = scratch
    odd = lax.rem(lax.axis_index("lon"), 2) == 1
    lat = lax.axis_index("lat")
    odd_lat = lax.rem(lat, 2) == 1
    at_top = lat == LAT - 1
    lane = iota(1)

    def place(j):
        if j < 6:
            return zq, j, q_ref, j
        if j < 18:
            return zf, 4 * ((j - 6) // 3) + j % 3, fields, j - 6
        if j == 18:
            return zq, 6, strip_ref, 0
        return zf, 4 * (j - 19) + 3, strip_ref, j - 18

    for j in range(TILES):
        ref, n, src, m = place(j)
        ref[n, pl.ds(BASE, 16), :] = src[m, pl.ds(BASE, 16), :]
        ref[n, pl.ds(32, 16), :] = src[m, pl.ds(NORTH - 16, 16), :]
        a, b = a_ref[pl.ds(4 * j, 4), :], b_ref[pl.ds(4 * j, 4), :]
        ref[n, pl.ds(BASE - 4, 4), :] = jnp.where(odd_lat, a, b)
        ref[n, pl.ds(48, 4), :] = jnp.where(odd_lat, b, a)

    own = [g_ref[pl.ds(8 * j, 8), :] for j in range(6)]
    strip = jnp.zeros((8, COLS), jnp.float32)
    for j in range(6):
        x, y = gx_ref[pl.ds(8 * j, 8), :], gy_ref[pl.ds(8 * j, 8), :]
        west, east = jnp.where(odd, x, y), jnp.where(odd, y, x)
        strip = jnp.where((lane >> 3) == j, roll(jnp.where(lane >= COLS - 4, west, own[j]), 8 * j + 4), strip)
        strip = jnp.where((lane >> 3) == j + 6, roll(jnp.where(lane < 4, east, own[j]), 8 * j + 52), strip)

    ghost = pl.ds(48, 1)

    def put(ref, s):
        @pl.when(at_top)
        def _():
            for j in range(6):
                ref[j, ghost, :] = own[j][s : s + 1, :]
            ref[6, ghost, :] = strip[s : s + 1, :]

    put(zq, 0)

    @pl.when(at_top)
    def _():
        for f, s in ((3, 4), (2, 5)):
            for l in range(LEVELS):
                zf[4 * f + l, ghost, :] = own[l][s : s + 1, :]
            zf[4 * f + 3, ghost, :] = strip[s : s + 1, :]

    for r in SOUTH_BLOCKS + NORTH_BLOCKS:

        def load(f, l, shift):
            return zf[4 * f + l, pl.ds(r + shift, 8), :]

        def store(n, l, x):
            zc[4 * n + l, pl.ds(r, 8), :] = x

        def with_edges(f, l, shift):
            return edges(load(f, 3, shift)) if l == 4 else load(f, l, shift)

        coef_block(with_edges, store)

    def loader(src, r):
        def load(j, shift):
            return edges(src[6, pl.ds(r, 8), :]) if j == 7 else src[j, pl.ds(r + shift, 8), :]

        return load

    def coefficient(r):
        return lambda n, l: zc[4 * n + l, pl.ds(r, 8), :]

    for s, (src, dst) in enumerate(((zq, zr), (zr, zq), (zq, zr))):
        for r in SOUTH_BLOCKS + NORTH_BLOCKS:
            out = advance(loader(src, r), coefficient(r), False)
            for j, x in enumerate(out[:7]):
                dst[j, pl.ds(r, 8), :] = x
        put(dst, s + 1)

    copies = []
    for z, (r, row) in enumerate(((16, 0), (40, ROWS - 8))):

        def store(n, l, x):
            patch[2 * n + z, l, :, :] = x

        out = advance(loader(zr, r), coefficient(r), True)
        outputs(out, lambda l: zf[12 + l, pl.ds(r, 8), :], store)
        for n, ref in enumerate((h_out, s_out, d_out)):
            copy = pltpu.make_async_copy(patch.at[2 * n + z], ref.at[:, pl.ds(row, 8), :], sems.at[2 * n + z])
            copy.start()
            copies.append(copy)
    for copy in copies:
        copy.wait()


def zones(q, fields, strip, a, b, g, gx, gy, *results):
    out = jax.ShapeDtypeStruct((LEVELS, ROWS, COLS), jnp.float32)
    anywhere = [pl.BlockSpec(memory_space=pl.ANY)] * 3
    return pl.pallas_call(
        zone_kernel,
        out_shape=(out, out, out),
        in_specs=vmem(8) + anywhere,
        out_specs=tuple(anywhere),
        scratch_shapes=[
            pltpu.VMEM((7, ZONE, COLS), jnp.float32),
            pltpu.VMEM((7, ZONE, COLS), jnp.float32),
            pltpu.VMEM((16, ZONE, COLS), jnp.float32),
            pltpu.VMEM((20, ZONE, COLS), jnp.float32),
            pltpu.VMEM((6, LEVELS, 8, COLS), jnp.float32),
            pltpu.SemaphoreType.DMA((6,)),
        ],
        input_output_aliases={8: 0, 9: 1, 10: 2},
        compiler_params=PARAMS,
        name="zones",
    )(q, fields, strip, a, b, g, gx, gy, *results)


def fold_exchange(message, seam):
    rotation = (seam[0] // COLS + 1 + lax.axis_index("lon")) % LON
    far = rotation >= HALF

    def relay(x):
        return lax.cond(far, lambda y: swap(y, PAIR_A), lambda y: y, x)

    branches = [functools.partial(swap, pairs=fold_pairs(r)) for r in range(HALF)]
    return relay(lax.switch(rotation % HALF, branches, relay(message)))


def on_device(t, s, u, v, k, w, seam):
    m = seam.reshape(1, COLS)
    xs, ys, pt, pc, q, fields = pack(t, s, u, v, k, w, m)
    yr = swap(ys, PAIR_Y)
    xr = swap(xs, PAIR_X)
    a, b, message = rows(q, fields, pt, pc, xs, xr, yr)
    partner = fold_exchange(message, seam)
    g = ghosts(partner, message, xr, yr)
    gy = swap(g, PAIR_Y)
    gx = swap(g, PAIR_X)
    a, b, _ = lax.optimization_barrier((a, b, g))
    br = swap(b, PAIR_B)
    ar = swap(a, PAIR_A)
    *results, strip = inner_steps(q, fields, pt, pc, xr, yr)
    return zones(q, fields, strip, ar, br, g, gx, gy, *results)


def solution(mesh):
    block = P(None, "lat", "lon")
    return jax.shard_map(
        on_device,
        mesh=mesh,
        in_specs=(block,) * 6 + (P("lon"),),
        out_specs=(block,) * 3,
        check_vma=False,
    )
```

time: 91.9 us -> 54.4 us (0.59)
  the two profiles are of different devices: /device:TPU:4 before, /device:TPU:1 now
where the time goes in v2:
time: 54.4 us; the launch traced here: 54.6 us
  starting transfers between devices  30.4 us (56%)
  Pallas kernels  16.4 us (30%)
  waiting for transfers between devices  6.26 us (12%)
  between operations  0.88 us (2%)
  local copies, waits for them, and re-layouts  0.64 us (1%)
    ppermute x9, starting transfers between devices, swap(): return lax.ppermute(x, AXES, pairs)  30.4 us
    pallas_call x1, Pallas kernels, inner_steps(): pl.pallas_call(main_kernel, out_shape=(out, out, out, jax.ShapeDtypeStruc...  9.66 us
    ppermute x9, waiting for transfers between devices, swap(): return lax.ppermute(x, AXES, pairs)  6.26 us
    pallas_call x1, Pallas kernels, pack(): pl.pallas_call(pack_kernel, out_shape=(edge, edge, own, own, jax.ShapeDty...  2.7 us
    pallas_call x1, Pallas kernels, zones(): pl.pallas_call(zone_kernel, out_shape=(out, out, out), in_specs=vmem(8) +...  2.38 us
    pallas_call x1, Pallas kernels, ghosts(): pl.pallas_call(ghost_kernel, out_shape=jax.ShapeDtypeStruct((48, COLS), j...  1.53 us
  transfers between devices with their start and end apart: 9, of which 4 were waited for; matrix products, arithmetic and copies ran while one was open for 0% of the time, Pallas kernels for 18%

profile of v2, /device:TPU:1, one launch (start us, length us, event | category | flops | bytes accessed | tf_op | source)
XLA Modules:
  0.0 54.6 jit_solution(104708123276635157)
XLA Ops:
  0.6 0.0 copy-start
  0.6 2.7 %pack.1 = (f32[272,128]{1,0:T(8,128)S(1)}, f32[272,128]{1,0:T(8,128)S(1)}, f32[256,128]{1,0:T(8,128)S(1)}, f32[256,128]{1,0:T(8,128)S(1)}, f32[6,288,128]{2,1,0:T(8,128)S(1)}, /*index=5*/f32[12,288,128]{2,1,0:T(8,128)S(1)}) custom-call(f32[3,256,128]{2,1,0:T(8,128)} %t_hbm.1, f32[3,256,128]{2,1,0:T(8,128)} %s_hbm.1, f32[3,256,128]{2,1,0:T(8,128)} %u_hbm.1, ...), custom_call_target="tpu_custom_call" | custom-call | tf_op jit(solution)/shard_map/pack/pallas_call | solution.py:135
  3.3 9.9 %collective-permute-start.35 = (f32[272,128]{1,0:T(8,128)S(1)}, f32[272,128]{1,0:T(8,128)S(1)}, u32[]{:S(2)}, u32[]{:S(2)}) collective-permute-start(f32[272,128]{1,0:T(8,128)S(1)} %get-tuple-element.98), channel_id=1, source_target_pairs={{0,252},{1,253},{2,254},{3,255},{4,8},{5,9},{6,10},{7,11},{8,4},{9... | collective-permute-start | bytes 417800 | tf_op jit(solution)/shard_map/ppermute | solution.py:48
  13.2 0.0 collective-permute-start.34
  13.2 0.0 copy-done
  13.4 3.2 %collective-permute-done.35.yr_ref.ye_ref = f32[272,128]{1,0:T(8,128)S(1)} collective-permute-done((f32[272,128]{1,0:T(8,128)S(1)}, f32[272,128]{1,0:T(8,128)S(1)}, u32[]{:S(2)}, u32[]{:S(2)}) %collective-permute-start.35) | collective-permute-done | bytes 139296 | tf_op jit(solution)/shard_map/ppermute | solution.py:48
  16.6 0.8 %collective-permute-done.34.xr_ref.xe_ref = f32[272,128]{1,0:T(8,128)S(1)} collective-permute-done((f32[272,128]{1,0:T(8,128)S(1)}, f32[272,128]{1,0:T(8,128)S(1)}, u32[]{:S(2)}, u32[]{:S(2)}) %collective-permute-start.34) | collective-permute-done | bytes 139296 | tf_op jit(solution)/shard_map/ppermute | solution.py:48
  17.4 0.2 rows.1
  17.6 3.0 %conditional.3 = (f32[192,128]{1,0:T(8,128)}) conditional(s32[]{:T(128)} %convert_element_type.4, f32[192,128]{1,0:T(8,128)S(1)} %get-tuple-element.102.d_ref, f32[192,128]{1,0:T(8,128)S(1)} %get-tuple-element.102.d_ref), branch_computations={%region_0.1_spmd, %region_1.2_spmd} | conditional | bytes 393264 | solution.py:605
  17.6 1.9 %collective-permute-start = (f32[192,128]{1,0:T(8,128)S(1)}, f32[192,128]{1,0:T(8,128)}, u32[]{:S(2)}, u32[]{:S(2)}) collective-permute-start(f32[192,128]{1,0:T(8,128)S(1)} %param.1), channel_id=1, source_target_pairs={{0,1},{1,0},{2,3},{3,2},{4,5},{5,4},{6,7},{7,6},{8,9},{9,8},{10,11... | collective-permute-start | bytes 294920 | tf_op jit(solution)/shard_map/cond/branch_1_fun/ppermute | solution.py:48
  19.5 1.1 %collective-permute-done = f32[192,128]{1,0:T(8,128)} collective-permute-done((f32[192,128]{1,0:T(8,128)S(1)}, f32[192,128]{1,0:T(8,128)}, u32[]{:S(2)}, u32[]{:S(2)}) %collective-permute-start) | collective-permute-done | bytes 98336 | tf_op jit(solution)/shard_map/cond/branch_1_fun/ppermute | solution.py:48
  20.6 1.3 %conditional.4 = (f32[192,128]{1,0:T(8,128)}) conditional(s32[]{:T(128)} %clamp.3, f32[192,128]{1,0:T(8,128)} %get-tuple-element.108, f32[192,128]{1,0:T(8,128)} %get-tuple-element.108, f32[192,128]{1,0:T(8,128)} %get-tuple-element.108, f32[192,128]{1,0:T(8,128)} %get-tuple-element.108, ...), branch_computations={%region_2.3_spmd, %region_3.4_spmd, %region_4.5_spmd, %region_5.6_... | conditional | bytes 393264 | solution.py:608
  20.6 1.3 %collective-permute-start.23 = (f32[192,128]{1,0:T(8,128)}, f32[192,128]{1,0:T(8,128)}, u32[]{:S(2)}, u32[]{:S(2)}) collective-permute-start(f32[192,128]{1,0:T(8,128)} %param.24), channel_id=1, source_target_pairs={{3,87},{7,83},{11,79},{15,75},{19,71},{23,67},{27,63},{31,59},{35,... | collective-permute-start | bytes 294920 | tf_op jit(solution)/shard_map/cond/branch_22_fun/ppermute | solution.py:48
  21.9 0.0 collective-permute-done.23
  21.9 2.1 %conditional.5 = (f32[192,128]{1,0:T(8,128)}) conditional(s32[]{:T(128)} %convert_element_type.4, f32[192,128]{1,0:T(8,128)} %get-tuple-element.109, f32[192,128]{1,0:T(8,128)} %get-tuple-element.109), branch_computations={%region_34.35_spmd, %region_35.36_spmd} | conditional | bytes 589872 | solution.py:605
  21.9 0.4 collective-permute-start.33
  22.3 1.2 %collective-permute-done.33 = f32[192,128]{1,0:T(8,128)S(1)} collective-permute-done((f32[192,128]{1,0:T(8,128)}, f32[192,128]{1,0:T(8,128)S(1)}, u32[]{:S(2)}, u32[]{:S(2)}) %collective-permute-start.33) | collective-permute-done | bytes 98336 | tf_op jit(solution)/shard_map/cond/branch_1_fun/ppermute | solution.py:48
  23.4 0.6 %copy.48 = f32[192,128]{1,0:T(8,128)} copy(f32[192,128]{1,0:T(8,128)S(1)} %collective-permute-done.33) | data formatting | bytes 196608 | tf_op jit(solution)/shard_map/cond
  24.0 1.5 %ghost.1.g_ref = f32[48,128]{1,0:T(8,128)S(1)} custom-call(f32[192,128]{1,0:T(8,128)} %get-tuple-element.110.p_ref, f32[192,128]{1,0:T(8,128)S(1)} %get-tuple-element.102.d_ref, f32[272,128]{1,0:T(8,128)S(1)} %collective-permute-done.34.xr_ref.xe_ref, f32[272,128]{1,0:T(8,128)S(1)} %collective-permute-done.35.yr_ref.ye_ref), custom_call_target="tpu_custom_call" | custom-call | tf_op jit(solution)/shard_map/ghost/pallas_call | solution.py:335
  25.6 0.4 collective-permute-start.36
  26.0 15.4 %collective-permute-start.37 = (f32[96,128]{1,0:T(8,128)S(1)}, f32[96,128]{1,0:T(8,128)S(1)}, u32[]{:S(2)}, u32[]{:S(2)}) collective-permute-start(f32[96,128]{1,0:T(8,128)S(1)} %get-tuple-element.104), channel_id=1, source_target_pairs={{1,2},{2,1},{5,6},{6,5},{9,10},{10,9},{13,14},{14,13},{17,18},{18,... | collective-permute-start | bytes 147464 | tf_op jit(solution)/shard_map/ppermute | solution.py:48
  41.4 1.1 %collective-permute-start.39 = (f32[48,128]{1,0:T(8,128)S(1)}, f32[48,128]{1,0:T(8,128)S(1)}, u32[]{:S(2)}, u32[]{:S(2)}) collective-permute-start(f32[48,128]{1,0:T(8,128)S(1)} %ghost.1.g_ref), channel_id=1, source_target_pairs={{0,252},{1,253},{2,254},{3,255},{4,8},{5,9},{6,10},{7,11},{8,4},{9... | collective-permute-start | bytes 73736 | tf_op jit(solution)/shard_map/ppermute | solution.py:48
  42.5 0.0 collective-permute-start.38
  42.5 9.7 %main.1 = (f32[3,256,128]{2,1,0:T(8,128)}, f32[3,256,128]{2,1,0:T(8,128)}, f32[3,256,128]{2,1,0:T(8,128)}, f32[5,288,128]{2,1,0:T(8,128)S(1)}) custom-call(f32[6,288,128]{2,1,0:T(8,128)S(1)} %get-tuple-element.93.q_ref, f32[12,288,128]{2,1,0:T(8,128)S(1)} %get-tuple-element.94.fields, f32[256,128]{1,0:T(8,128)S(1)} %get-tuple-element.95.pt_ref, ...), custom_call_target="tpu_custom_call" | custom-call | flops 60000000 | bytes 36000000 | tf_op jit(solution)/shard_map/main/pallas_call | solution.py:459
  52.2 0.0 collective-permute-done.39.gy_ref
  52.2 0.0 collective-permute-done.38.gx_ref
  52.2 0.0 collective-permute-done.36.a_ref
  52.2 0.0 collective-permute-done.37.b_ref
  52.2 2.4 %zones.1 = (f32[3,256,128]{2,1,0:T(8,128)}, f32[3,256,128]{2,1,0:T(8,128)}, f32[3,256,128]{2,1,0:T(8,128)}) custom-call(f32[6,288,128]{2,1,0:T(8,128)S(1)} %get-tuple-element.93.q_ref, f32[12,288,128]{2,1,0:T(8,128)S(1)} %get-tuple-element.94.fields, ...), custom_call_target="tpu_custom_call", output_to_operand_aliasing={{0}: (8, {}), {1}: (9, {}), {2}: (10, {})} | custom-call | tf_op jit(solution)/shard_map/zones/pallas_call | solution.py:581
Async XLA Ops:
  0.6 12.6 %copy-start = (s32[128]{0:T(128)S(1)}, s32[128]{0:T(128)}, u32[]{:S(2)}) copy-start(s32[128]{0:T(128)} %param.49) | copy-start | bytes 1540
  3.3 13.3 %collective-permute-start.35 = (f32[272,128]{1,0:T(8,128)S(1)}, f32[272,128]{1,0:T(8,128)S(1)}, u32[]{:S(2)}, u32[]{:S(2)}) collective-permute-start(f32[272,128]{1,0:T(8,128)S(1)} %get-tuple-element.98), channel_id=1, source_target_pairs={{0,252},{1,253},{2,254},{3,255},{4,8},{5,9},{6,10},{7,11},{8,4},{9... | collective-permute-start | bytes 417800 | tf_op jit(solution)/shard_map/ppermute | solution.py:48
  13.2 4.2 %collective-permute-start.34 = (f32[272,128]{1,0:T(8,128)S(1)}, f32[272,128]{1,0:T(8,128)S(1)}, u32[]{:S(2)}, u32[]{:S(2)}) collective-permute-start(f32[272,128]{1,0:T(8,128)S(1)} %get-tuple-element.97.xs_ref), channel_id=1, source_target_pairs={{0,4},{1,5},{2,6},{3,7},{4,0},{5,1},{6,2},{7,3},{8,12},{9,13},{10,... | collective-permute-start | bytes 417800 | tf_op jit(solution)/shard_map/ppermute | solution.py:48
  17.6 3.0 %collective-permute-start = (f32[192,128]{1,0:T(8,128)S(1)}, f32[192,128]{1,0:T(8,128)}, u32[]{:S(2)}, u32[]{:S(2)}) collective-permute-start(f32[192,128]{1,0:T(8,128)S(1)} %param.1), channel_id=1, source_target_pairs={{0,1},{1,0},{2,3},{3,2},{4,5},{5,4},{6,7},{7,6},{8,9},{9,8},{10,11... | collective-permute-start | bytes 294920 | tf_op jit(solution)/shard_map/cond/branch_1_fun/ppermute | solution.py:48
  20.6 1.3 %collective-permute-start.23 = (f32[192,128]{1,0:T(8,128)}, f32[192,128]{1,0:T(8,128)}, u32[]{:S(2)}, u32[]{:S(2)}) collective-permute-start(f32[192,128]{1,0:T(8,128)} %param.24), channel_id=1, source_target_pairs={{3,87},{7,83},{11,79},{15,75},{19,71},{23,67},{27,63},{31,59},{35,... | collective-permute-start | bytes 294920 | tf_op jit(solution)/shard_map/cond/branch_22_fun/ppermute | solution.py:48
  21.9 1.5 %collective-permute-start.33 = (f32[192,128]{1,0:T(8,128)}, f32[192,128]{1,0:T(8,128)S(1)}, u32[]{:S(2)}, u32[]{:S(2)}) collective-permute-start(f32[192,128]{1,0:T(8,128)} %param.35), channel_id=1, source_target_pairs={{0,1},{1,0},{2,3},{3,2},{4,5},{5,4},{6,7},{7,6},{8,9},{9,8},{10,11... | collective-permute-start | bytes 294920 | tf_op jit(solution)/shard_map/cond/branch_1_fun/ppermute | solution.py:48
  25.6 26.6 %collective-permute-start.36 = (f32[96,128]{1,0:T(8,128)S(1)}, f32[96,128]{1,0:T(8,128)S(1)}, u32[]{:S(2)}, u32[]{:S(2)}) collective-permute-start(f32[96,128]{1,0:T(8,128)S(1)} %get-tuple-element.103), channel_id=1, source_target_pairs={{0,1},{1,0},{2,3},{3,2},{4,5},{5,4},{6,7},{7,6},{8,9},{9,8},{10,11... | collective-permute-start | bytes 147464 | tf_op jit(solution)/shard_map/ppermute | solution.py:48
  26.0 26.2 %collective-permute-start.37 = (f32[96,128]{1,0:T(8,128)S(1)}, f32[96,128]{1,0:T(8,128)S(1)}, u32[]{:S(2)}, u32[]{:S(2)}) collective-permute-start(f32[96,128]{1,0:T(8,128)S(1)} %get-tuple-element.104), channel_id=1, source_target_pairs={{1,2},{2,1},{5,6},{6,5},{9,10},{10,9},{13,14},{14,13},{17,18},{18,... | collective-permute-start | bytes 147464 | tf_op jit(solution)/shard_map/ppermute | solution.py:48
  41.4 10.7 %collective-permute-start.39 = (f32[48,128]{1,0:T(8,128)S(1)}, f32[48,128]{1,0:T(8,128)S(1)}, u32[]{:S(2)}, u32[]{:S(2)}) collective-permute-start(f32[48,128]{1,0:T(8,128)S(1)} %ghost.1.g_ref), channel_id=1, source_target_pairs={{0,252},{1,253},{2,254},{3,255},{4,8},{5,9},{6,10},{7,11},{8,4},{9... | collective-permute-start | bytes 73736 | tf_op jit(solution)/shard_map/ppermute | solution.py:48
  42.5 9.7 %collective-permute-start.38 = (f32[48,128]{1,0:T(8,128)S(1)}, f32[48,128]{1,0:T(8,128)S(1)}, u32[]{:S(2)}, u32[]{:S(2)}) collective-permute-start(f32[48,128]{1,0:T(8,128)S(1)} %ghost.1.g_ref), channel_id=1, source_target_pairs={{0,4},{1,5},{2,6},{3,7},{4,0},{5,1},{6,2},{7,3},{8,12},{9,13},{10,... | collective-permute-start | bytes 73736 | tf_op jit(solution)/shard_map/ppermute | solution.py:48
